TPU v7x, 32 devices: a whole 2x2x4 slice. The times are simulated.
32 devices in a mesh: row: 8 (over z, x), col: 4 (over y, core).
Axes of the slice: x: 2, y: 2, z: 4, core: 2. Of those that a mesh axis runs over, the one named last changes fastest.
Arguments:
- volt_start: float32 [2, 256, 1024], P(None, 'row', 'col'), may hold values from 0.6 to 1.2
- cap_dt: float32 [2, 256, 1024], P(None, 'row', 'col'), may hold values from 0.1 to 1
- wire_cond: float32 [2, 256, 1024], P(None, 'row', 'col'), may hold values from 0.5 to 2
- via_cond: float32 [256, 1024], P('row', 'col'), may hold values from 0.2 to 2
- load_current: float32 [256, 1024], P('row', 'col'), may hold values from 0.05 to 0.5
- load_wave: float32 [1], replicated, may hold values from 0.5 to 1.5
- decap_state: float32 [256, 1024], P('row', 'col'), may hold values from 0.6 to 1.2
- decap_cond: float32 [256, 1024], P('row', 'col'), may hold values from 0.1 to 2
- bump_map: int32 [256, 1024], P('row', 'col'), may hold values from 0 to 8191, as said below
- via_mask: int32 [256, 1024], P('row', 'col'), may hold values 0 or 1
- bump_cond: float32 [8192], replicated, may hold values from 0.4 to 0.8
- bump_supply: float32 [8192], replicated, may hold values from 0.5 to 1.5
- package: float32 [8192, 8192], P(('row', 'col')), may hold values from -0.0625 to 0.0625, as said below
Outputs:
- voltage: float32 [2, 256, 1024], P(None, 'row', 'col')
- decap_volt: float32 [256, 1024], P('row', 'col')
- bump_volt: float32 [8192], P(('row', 'col'))
Inputs may be any that keep to these rules, and one draw needn't show every extreme that they name: bump_map[i, j] = min((i + s) // 2, 127) * 64 + j // 16, with an integer s drawn for each node, 0 <= s <= 256 / 128 / 4. package is symmetric.
All inputs are finite; a program needn't handle non-finite values. No bound on the sum of `via_mask` on one device may be relied on, other than what follows from the above.
Results may differ from a plain program's by a relative error of at most 0.0001.
Values sent between devices are 32-bit elements; how exact they have to be, the bound alone decides.
No kernel may reach another device: no remote copies, remote signals or barrier semaphores. Data moves between devices by JAX's collectives and lax.ppermute only.
A program may use at most 64 MiB of HBM per device.

v0:
```python
import jax
import jax.numpy as jnp
import numpy as np
from jax import lax
from jax.sharding import PartitionSpec as P

BR = 128
BC = 64
DEG = 4


CHEB_LO = 0.05
CHEB_HI = 2.0
CHEB_MID = (CHEB_HI + CHEB_LO) / 2.0
CHEB_HALF = (CHEB_HI - CHEB_LO) / 2.0
CHEB_RATIO = CHEB_MID / CHEB_HALF


def from_behind(array, axis, by):
    peers = lax.axis_size(axis)
    pairs = [(i, i + by) for i in range(peers) if 0 <= i + by < peers]
    return lax.ppermute(array, axis, pairs)


def padded_2(block, sides, width):
    for axis, dim in sides:
        count = lax.axis_size(axis)
        forward = [(i, i + 1) for i in range(count - 1)]
        backward = [(target, source) for source, target in forward]
        low = lax.ppermute(
            lax.slice_in_dim(block, block.shape[dim] - width, None, axis=dim), axis, forward
        )
        high = lax.ppermute(lax.slice_in_dim(block, 0, width, axis=dim), axis, backward)
        block = jnp.concatenate([low, block, high], axis=dim)
    return block


def chebyshev(iterate, source, diagonal, apply_matrix):
    residual = source - apply_matrix(iterate)
    direction = residual / (CHEB_MID * diagonal)
    rho_now = 1.0 / CHEB_RATIO
    for sweep in range(DEG):
        iterate = iterate + direction
        if sweep < DEG - 1:
            residual = residual - apply_matrix(direction)
            rho_next = 1.0 / (2.0 * CHEB_RATIO - rho_now)
            direction = (
                rho_next * rho_now * direction + 2.0 * rho_next / CHEB_HALF * residual / diagonal
            )
            rho_now = rho_next
    return iterate


def operate(padded, coefficients, coupled_volt):
    top_layer = padded[0, 1:-1, 1:-1]
    low_layer = padded[1, 1:-1, 1:-1]
    top_out = (
        coefficients[0] * top_layer
        - coefficients[2] * padded[0, 1:-1, 2:]
        - coefficients[3] * padded[0, 1:-1, :-2]
        - coefficients[6] * low_layer
        - coefficients[7] * coupled_volt
    )
    low_out = (
        coefficients[1] * low_layer
        - coefficients[4] * padded[1, 2:, 1:-1]
        - coefficients[5] * padded[1, :-2, 1:-1]
        - coefficients[6] * top_layer
    )
    return jnp.stack([top_out, low_out])


def spread(tile, lattice_rel, col_rel):
    columns = jnp.take(tile, jnp.asarray(col_rel, jnp.int32), axis=1)
    expanded = jnp.zeros(lattice_rel.shape, jnp.float32)
    for level in range(tile.shape[0]):
        expanded = jnp.where(lattice_rel == level, columns[level][None, :], expanded)
    return expanded


def shards(
    volt_start,
    cap_dt,
    wire_cond,
    via_cond,
    load_current,
    load_wave,
    decap_state,
    decap_cond,
    bump_map,
    via_mask,
    bump_cond,
    bump_supply,
    package,
):
    height, breadth = via_cond.shape
    row_count = lax.axis_size("row")
    col_count = lax.axis_size("col")
    row_index = lax.axis_index("row")
    col_index = lax.axis_index("col")
    bump_count = bump_cond.shape[0]
    block_rows = BR // row_count
    block_cols = BC // col_count
    tile_rows = height // block_rows
    tile_cols = breadth // block_cols
    reach = max(1, tile_rows // 4)
    row_base = row_index * block_rows
    col_base = col_index * block_cols
    row_position = lax.broadcasted_iota(jnp.int32, (height, breadth), 0)
    col_position = lax.broadcasted_iota(jnp.int32, (height, breadth), 1)
    link_row = jnp.where(
        (col_index == col_count - 1) & (col_position == breadth - 1), 0.0, wire_cond[0]
    )
    link_col = jnp.where(
        (row_index == row_count - 1) & (row_position == height - 1), 0.0, wire_cond[1]
    )
    node_cond = via_mask.astype(jnp.float32) * jnp.take(bump_cond, bump_map)
    supply_node = node_cond * jnp.take(bump_supply, bump_map)
    decap_frac = decap_cond / (1.0 + decap_cond)
    own_lattice = bump_map // BC - row_base

    def local_pieces(top_layer):
        weighted = node_cond * top_layer
        levels = []
        for level in range(block_rows + 1):
            picked = jnp.where(own_lattice == level, weighted, 0.0)
            levels.append(picked.reshape(height, block_cols, tile_cols).sum(axis=(0, 2)))
        return jnp.stack(levels)

    def bump_totals(top_layer):
        pieces = local_pieces(top_layer)
        canvas = jnp.zeros((BR + 1, BC), jnp.float32)
        canvas = lax.dynamic_update_slice(canvas, pieces, (row_base, col_base))
        return lax.psum(canvas[:BR].reshape(-1), ("row", "col"))

    def coupled_tile(totals, win_rows, win_cols, package_cols):
        return jnp.dot(totals, package_cols, precision=lax.Precision.HIGHEST).reshape(
            win_rows, win_cols
        )

    above = (0 + tile_rows - 1) // tile_rows
    below = (height + 0 - 1 + reach) // tile_rows
    left = (0 + tile_cols - 1) // tile_cols
    right = (breadth + 0 - 1) // tile_cols
    window_col_rel = (np.arange(breadth + 2 * 0) - 0) // tile_cols + left
    above, win_rows, left, win_cols, col_rel = (
        above,
        below + above + 1,
        left,
        right + left + 1,
        window_col_rel,
    )
    dest_row = np.arange(row_count)[:, None, None, None]
    dest_col = np.arange(col_count)[None, :, None, None]
    level = np.arange(win_rows)[None, None, :, None]
    offset = np.arange(win_cols)[None, None, None, :]
    lattice_row = np.clip(dest_row * block_rows - above + level, 0, BR - 1)
    lattice_col = np.clip(dest_col * block_cols - left + offset, 0, BC - 1)
    table = (lattice_row * BC + lattice_col).reshape(-1)
    picked = jnp.take(package, jnp.asarray(table, jnp.int32), axis=1)
    picked = picked.reshape(package.shape[0], row_count, col_count, win_rows * win_cols).transpose(
        1, 2, 0, 3
    )
    moved = lax.all_to_all(
        lax.all_to_all(picked, "row", split_axis=0, concat_axis=0, tiled=True),
        "col",
        split_axis=1,
        concat_axis=1,
        tiled=True,
    )
    package_cols = moved.reshape(bump_count, win_rows * win_cols)
    left_edge = from_behind(link_row[:, breadth - 1 :], "col", 1)
    left_link = jnp.concatenate([left_edge, link_row[:, :-1]], axis=1)
    up_edge = from_behind(link_col[height - 1 :, :], "row", 1)
    up_link = jnp.concatenate([up_edge, link_col[:-1, :]], axis=0)
    diag_top = cap_dt[0] + link_row + left_link + via_cond + node_cond
    diag_low = cap_dt[1] + link_col + up_link + via_cond + decap_frac
    diagonal = jnp.stack([diag_top, diag_low])
    coefficients = (diag_top, diag_low, link_row, left_link, link_col, up_link, via_cond, node_cond)
    lattice_rel = own_lattice + above

    def apply_matrix(iterate):
        tile = coupled_tile(bump_totals(iterate[0]), win_rows, win_cols, package_cols)
        coupled_volt = spread(tile, lattice_rel, col_rel)
        padded = padded_2(iterate, (("row", 1), ("col", 2)), 1)
        return operate(padded, coefficients, coupled_volt)

    voltage = volt_start
    decap_volt = decap_state
    source = jnp.stack(
        [
            cap_dt[0] * voltage[0] + supply_node,
            cap_dt[1] * voltage[1] + decap_frac * decap_volt - load_wave[0] * load_current,
        ]
    )
    voltage = chebyshev(voltage, source, diagonal, apply_matrix)
    decap_volt = (decap_volt + decap_cond * voltage[1]) / (1.0 + decap_cond)
    final_totals = bump_totals(voltage[0])
    per_device = package.shape[0]
    first_bump = (row_index * col_count + col_index) * per_device
    own_supply = lax.dynamic_slice_in_dim(bump_supply, first_bump, per_device)
    bump_volt = own_supply + jnp.dot(package, final_totals, precision=lax.Precision.HIGHEST)
    return (voltage, decap_volt, bump_volt)


def solution(mesh):
    placed = (
        P(None, "row", "col"),
        P(None, "row", "col"),
        P(None, "row", "col"),
        P("row", "col"),
        P("row", "col"),
        P(),
        P("row", "col"),
        P("row", "col"),
        P("row", "col"),
        P("row", "col"),
        P(),
        P(),
        P(("row", "col"), None),
    )
    return jax.shard_map(
        shards,
        mesh=mesh,
        in_specs=placed,
        out_specs=(P(None, "row", "col"), P("row", "col"), P(("row", "col"))),
        check_vma=False,
    )
```

profile of v0, /device:TPU:0, one launch (start us, length us, event | category | flops | bytes accessed | tf_op | source)
XLA Modules:
  0.0 817.8 jit_solution(17041327407624414809)
XLA Ops:
  0.7 9.0 %copy.28 = f32[256,8192]{0,1:T(8,128)} copy(f32[256,8192]{1,0:T(8,128)} %param.34) | data formatting | bytes 16777216 | tf_op args[12]
  9.7 24.7 %gather_fusion = f32[8704,256]{1,0:T(8,128)} fusion(f32[256,8192]{0,1:T(8,128)} %copy.28, s32[9216]{0:T(1024)S(1)} %pad_clamp_fusion), kind=kCustom, calls=%fused_computation.6 | custom fusion | bytes 17860608 | tf_op jit(solution)/shard_map/jit(_take)/gather | solution.py:160
  34.4 12.7 %copy.38 = f32[256,8,4,272]{0,2,3,1:T(4,128)} copy(f32[256,8,4,272]{0,3,2,1:T(8,128)} %bitcast.424) | data formatting | bytes 17825792 | tf_op jit(solution)/shard_map/jit(_take)/gather | solution.py:160
  47.1 202.1 %all_to_all.10 = f32[8,4,256,272]{2,1,3,0:T(4,128)S(1)} all-to-all(f32[8,4,256,272]{2,1,3,0:T(4,128)} %bitcast.425), channel_id=1, replica_groups=mesh['row'=8,'col'=4] {'row'}, dimensions={0} | all-to-all | bytes 17825792 | tf_op jit(solution)/shard_map/all_to_all | solution.py:165
  249.2 8.6 %copy.30 = f32[8,4,256,272]{2,0,3,1:T(8,128)} copy(f32[8,4,256,272]{2,1,3,0:T(4,128)S(1)} %all_to_all.10) | data formatting | bytes 17825792 | tf_op jit(solution)/shard_map/all_to_all | solution.py:165
  257.8 5.9 all-to-all-start.1
  263.8 3.4 collective-permute-start.5
  267.2 3.0 collective-permute-start.1
  273.5 45.5 %gather_fusion.1 = f32[8192]{0:T(1024)S(1)} fusion(f32[8192]{0:T(1024)S(1)} %copy-done, s32[8192]{0:T(1024)S(1)} %broadcast_clamp_fusion), kind=kCustom, calls=%fused_computation.clone | custom fusion | bytes 98304 | tf_op jit(solution)/shard_map/jit(_take)/gather | solution.py:117
  319.2 45.5 %gather_fusion.2 = f32[8192]{0:T(1024)S(1)} fusion(f32[8192]{0:T(1024)S(1)} %copy-done.2, s32[8192]{0:T(1024)S(1)} %broadcast_clamp_fusion), kind=kCustom, calls=%fused_computation.2.clone | custom fusion | bytes 98304 | tf_op jit(solution)/shard_map/jit(_take)/gather | solution.py:118
  371.5 5.0 collective-permute-start.4
  376.5 40.9 %psum.35 = f32[8192]{0:T(1024)S(1)} all-reduce(f32[8192]{0:T(1024)S(1)} %reshape.224), channel_id=1, replica_groups=mesh['row'=8,'col'=4] {'row','col'}, use_global_device_ids=true, to_apply=%region_34.36 | all-reduce | flops 8192 | bytes 65536 | tf_op jit(solution)/shard_map/psum | solution.py:134
  417.4 12.7 %copy.31 = f32[8,4,256,272]{2,1,0,3:T(4,128)} copy(f32[8,4,256,272]{2,0,3,1:T(8,128)} %all-to-all-done.1) | data formatting | bytes 17825792 | tf_op jit(solution)/shard_map/all_to_all | solution.py:164
  430.2 11.7 %reshape.225 = f32[8192,272]{0,1:T(8,128)} reshape(f32[8,4,256,272]{2,1,0,3:T(4,128)} %copy.31) | data formatting | bytes 17825792 | tf_op jit(solution)/shard_map/reshape | solution.py:171
  441.8 32.4 %fusion.103 = f32[1,17,16]{2,0,1:T(1,128)S(1)} fusion(f32[8192,1,1]{0,1,2:T(1,128)S(1)} %bitcast.443, f32[17,16,8192]{2,1,0:T(8,128)} %bitcast.416), kind=kOutput, calls=%fused_computation.362 | convolution fusion | flops 26738688 | bytes 8946752 | tf_op jit(solution)/shard_map/dot_general | solution.py:137
  476.5 4.2 collective-permute-start.6
  482.0 4.2 collective-permute-done.7
  490.6 41.0 %psum.36 = f32[8192]{0:T(1024)S(1)} all-reduce(f32[8192]{0:T(1024)S(1)} %reshape.226), channel_id=1, replica_groups=mesh['row'=8,'col'=4] {'row','col'}, use_global_device_ids=true, to_apply=%region_69.72 | all-reduce | flops 8192 | bytes 65536 | tf_op jit(solution)/shard_map/psum | solution.py:134
  531.6 32.2 %fusion.104 = f32[1,17,16]{2,0,1:T(1,128)S(1)} fusion(f32[8192,1,1]{0,1,2:T(1,128)S(1)} %bitcast.445, f32[17,16,8192]{2,1,0:T(8,128)} %bitcast.417), kind=kOutput, calls=%fused_computation.363 | convolution fusion | flops 26738688 | bytes 8946752 | tf_op jit(solution)/shard_map/dot_general | solution.py:137
  566.1 3.0 collective-permute-start.9
  570.6 4.2 collective-permute-start.10
  576.1 4.2 collective-permute-done.11
  584.9 42.2 %psum.37 = f32[8192]{0:T(1024)S(1)} all-reduce(f32[8192]{0:T(1024)S(1)} %reshape.227), channel_id=1, replica_groups=mesh['row'=8,'col'=4] {'row','col'}, use_global_device_ids=true, to_apply=%region_104.107 | all-reduce | flops 8192 | bytes 65536 | tf_op jit(solution)/shard_map/psum | solution.py:134
  627.1 32.2 %fusion.105 = f32[1,17,16]{2,0,1:T(1,128)S(1)} fusion(f32[8192,1,1]{0,1,2:T(1,128)S(1)} %bitcast.446, f32[17,16,8192]{2,1,0:T(8,128)} %bitcast.418), kind=kOutput, calls=%fused_computation.364 | convolution fusion | flops 26738688 | bytes 8946752 | tf_op jit(solution)/shard_map/dot_general | solution.py:137
  661.5 3.0 collective-permute-start.13
  666.0 4.2 collective-permute-start.14
  671.7 3.9 collective-permute-done.15
  680.1 42.1 %psum.38 = f32[8192]{0:T(1024)S(1)} all-reduce(f32[8192]{0:T(1024)S(1)} %reshape.228), channel_id=1, replica_groups=mesh['row'=8,'col'=4] {'row','col'}, use_global_device_ids=true, to_apply=%region_139.142 | all-reduce | flops 8192 | bytes 65536 | tf_op jit(solution)/shard_map/psum | solution.py:134
  722.2 32.2 %fusion.106 = f32[1,17,16]{2,0,1:T(1,128)S(1)} fusion(f32[8192,1,1]{0,1,2:T(1,128)S(1)} %bitcast.444, f32[17,16,8192]{2,1,0:T(8,128)} %bitcast.419), kind=kOutput, calls=%fused_computation.365 | convolution fusion | flops 26738688 | bytes 8946752 | tf_op jit(solution)/shard_map/dot_general | solution.py:137
  756.7 3.3 collective-permute-start.17
  766.5 41.5 %psum.39 = f32[8192]{0:T(1024)S(1)} all-reduce(f32[8192]{0:T(1024)S(1)} %reshape.229), channel_id=1, replica_groups=mesh['row'=8,'col'=4] {'row','col'}, use_global_device_ids=true, to_apply=%region_174.177 | all-reduce | flops 8192 | bytes 65536 | tf_op jit(solution)/shard_map/psum | solution.py:134
  808.0 8.9 %fusion.107 = f32[1,256]{1,0:T(1,128)S(1)} fusion(f32[8192,1]{0,1:T(1,128)S(1)} %bitcast.447, f32[256,8192]{1,0:T(8,128)} %param.34), kind=kOutput, calls=%fused_computation.366 | convolution fusion | flops 25165824 | bytes 8422400 | tf_op jit(solution)/shard_map/dot_general | solution.py:202
  (307 shorter events, 45.6 us)
Async XLA Ops:
  0.6 272.9 %copy-start = (f32[8192]{0:T(1024)S(1)}, f32[8192]{0:T(1024)}, u32[]{:S(2)}) copy-start(f32[8192]{0:T(1024)} %param.32) | copy-start | bytes 98308
  257.8 9.4 %copy-start.3 = (f32[2,32,256]{2,1,0:T(8,128)S(1)}, f32[2,32,256]{2,1,0:T(8,128)}, u32[]{:S(2)}) copy-start(f32[2,32,256]{2,1,0:T(8,128)} %param.22) | copy-start | bytes 196612
  257.8 15.6 %copy-start.9 = (s32[32,256]{1,0:T(8,128)S(1)}, s32[32,256]{1,0:T(8,128)}, u32[]{:S(2)}) copy-start(s32[32,256]{1,0:T(8,128)} %param.30) | copy-start | bytes 98308
  257.8 159.6 %all-to-all-start.1 = ((f32[8,4,256,272]{2,0,3,1:T(8,128)}), f32[8,4,256,272]{2,0,3,1:T(8,128)}, u32[]{:S(2)}, u32[]{:S(2)}) async-start(f32[8,4,256,272]{2,0,3,1:T(8,128)} %copy.30), calls=%async_computation.1 | async-start | bytes 17825792 | tf_op jit(solution)/shard_map/all_to_all | solution.py:164
  263.8 101.7 %collective-permute-start.5 = (f32[1,256]{1,0:T(1,128)S(1)}, f32[1,256]{1,0:T(1,128)S(1)}, u32[]{:S(2)}, u32[]{:S(2)}) collective-permute-start(f32[1,256]{1,0:T(1,128)S(1)} %slice.552), channel_id=1, source_target_pairs={{0,4},{4,8},{8,12},{12,16},{16,20},{20,24},{24,28},{1,5},{5,9},{9,... | collective-permute-start | bytes 3080 | tf_op jit(solution)/shard_map/ppermute | solution.py:22
  267.2 98.3 %collective-permute-start.1 = (f32[2,1,256]{2,1,0:T(1,128)S(1)}, f32[2,1,256]{2,1,0:T(1,128)S(1)}, u32[]{:S(2)}, u32[]{:S(2)}) collective-permute-start(f32[2,1,256]{2,1,0:T(1,128)S(1)} %get-tuple-element.208), channel_id=1, source_target_pairs={{0,4},{4,8},{8,12},{12,16},{16,20},{20,24},{24,28},{1,5},{5,9},{9,... | collective-permute-start | bytes 6152 | tf_op jit(solution)/shard_map/ppermute | solution.py:30
  270.2 95.3 %collective-permute-start.2 = (f32[2,1,256]{2,1,0:T(1,128)S(1)}, f32[2,1,256]{2,1,0:T(1,128)S(1)}, u32[]{:S(2)}, u32[]{:S(2)}) collective-permute-start(f32[2,1,256]{2,1,0:T(1,128)S(1)} %get-tuple-element.207), channel_id=1, source_target_pairs={{4,0},{8,4},{12,8},{16,12},{20,16},{24,20},{28,24},{5,1},{9,5},{13... | collective-permute-start | bytes 6152 | tf_op jit(solution)/shard_map/ppermute | solution.py:33
  271.6 93.8 %collective-permute-start = (f32[32,1]{1,0:T(8,128)S(1)}, f32[32,1]{1,0:T(8,128)S(1)}, u32[]{:S(2)}, u32[]{:S(2)}) collective-permute-start(f32[32,1]{1,0:T(8,128)S(1)} %slice.530), channel_id=1, source_target_pairs={{0,1},{1,2},{2,3},{4,5},{5,6},{6,7},{8,9},{9,10},{10,11},{12,13},{... | collective-permute-start | bytes 392 | tf_op jit(solution)/shard_map/ppermute | solution.py:22
  273.5 45.6 %copy-start.2 = (f32[8192]{0:T(1024)S(1)}, f32[8192]{0:T(1024)}, u32[]{:S(2)}) copy-start(f32[8192]{0:T(1024)} %param.33) | copy-start | bytes 98308
  319.1 46.3 %copy-start.14 = (s32[256]{0:T(256)S(1)}, s32[256]{0:T(256)}, u32[]{:S(2)}) copy-start(s32[256]{0:T(256)} %constant.178) | copy-start | bytes 3076
  319.1 46.3 %copy-start.5 = (f32[2,32,256]{2,1,0:T(8,128)S(1)}, f32[2,32,256]{2,1,0:T(8,128)}, u32[]{:S(2)}) copy-start(f32[2,32,256]{2,1,0:T(8,128)} %param.23) | copy-start | bytes 196612
  319.1 46.3 %copy-start.13 = (s32[32,256]{1,0:T(8,128)S(1)}, s32[32,256]{1,0:T(8,128)}, u32[]{:S(2)}) copy-start(s32[32,256]{1,0:T(8,128)} %param.31) | copy-start | bytes 98308
  319.1 46.3 %copy-start.4 = (f32[32,256]{1,0:T(8,128)S(1)}, f32[32,256]{1,0:T(8,128)}, u32[]{:S(2)}) copy-start(f32[32,256]{1,0:T(8,128)} %param.25) | copy-start | bytes 98308
  319.1 46.5 %copy-start.7 = (f32[32,256]{1,0:T(8,128)S(1)}, f32[32,256]{1,0:T(8,128)}, u32[]{:S(2)}) copy-start(f32[32,256]{1,0:T(8,128)} %param.29) | copy-start | bytes 98308
  319.1 46.4 %copy-start.8 = (f32[32,256]{1,0:T(8,128)S(1)}, f32[32,256]{1,0:T(8,128)}, u32[]{:S(2)}) copy-start(f32[32,256]{1,0:T(8,128)} %param.28) | copy-start | bytes 98308
  319.1 46.4 %copy-start.12 = (f32[32,256]{1,0:T(8,128)S(1)}, f32[32,256]{1,0:T(8,128)}, u32[]{:S(2)}) copy-start(f32[32,256]{1,0:T(8,128)} %param.26) | copy-start | bytes 98308
  370.2 106.1 %collective-permute-start.3 = (f32[2,34,1]{2,1,0:T(8,128)S(1)}, f32[2,34,1]{2,1,0:T(8,128)S(1)}, u32[]{:S(2)}, u32[]{:S(2)}) collective-permute-start(f32[2,34,1]{2,1,0:T(8,128)S(1)} %get-tuple-element.188), channel_id=1, source_target_pairs={{1,0},{2,1},{3,2},{5,4},{6,5},{7,6},{9,8},{10,9},{11,10},{13,12},{... | collective-permute-start | bytes 824 | tf_op jit(solution)/shard_map/ppermute | solution.py:33
  371.5 104.9 %collective-permute-start.4 = (f32[2,34,1]{2,1,0:T(8,128)S(1)}, f32[2,34,1]{2,1,0:T(8,128)S(1)}, u32[]{:S(2)}, u32[]{:S(2)}) collective-permute-start(f32[2,34,1]{2,1,0:T(8,128)S(1)} %get-tuple-element.189), channel_id=1, source_target_pairs={{0,1},{1,2},{2,3},{4,5},{5,6},{6,7},{8,9},{9,10},{10,11},{12,13},{... | collective-permute-start | bytes 824 | tf_op jit(solution)/shard_map/ppermute | solution.py:30
  476.5 5.5 collective-permute-start.6
  480.7 5.5 collective-permute-start.7
  564.8 5.6 collective-permute-start.8
  566.1 4.3 collective-permute-start.9
  570.6 5.5 collective-permute-start.10
  574.8 5.5 collective-permute-start.11
  660.2 5.6 collective-permute-start.12
  661.5 4.3 collective-permute-start.13
  666.0 5.7 collective-permute-start.14
  670.2 5.5 collective-permute-start.15
  722.2 95.3 %copy-start.1 = (f32[8192]{0:T(1024)S(1)}, f32[8192]{0:T(1024)}, u32[]{:S(2)}) copy-start(f32[8192]{0:T(1024)} %param.32) | copy-start | bytes 98308
  755.4 5.8 collective-permute-start.16
  756.7 4.5 collective-permute-start.17
  761.5 56.1 %copy-start.6 = (f32[2,32,256]{2,1,0:T(8,128)}, f32[2,32,256]{2,1,0:T(8,128)S(1)}, u32[]{:S(2)}) copy-start(f32[2,32,256]{2,1,0:T(8,128)S(1)} %fusion.3) | copy-start | bytes 196612
  (2 other events, 14.9 us)
where the time goes:
time: 825 us; the launch traced here: 818 us
  blocking collectives  410 us (50%)
  local copies, waits for them, and re-layouts  190 us (23%)
  matrix products  138 us (17%)
  starting transfers between devices  51.4 us (6%)
  other arithmetic  13.4 us (2%)
  waiting for transfers between devices  12.3 us (1%)
    psum x5, blocking collectives, bump_totals(): return lax.psum(canvas[:BR].reshape(-1), ('row', 'col'))  208 us
    all_to_all x1, blocking collectives, shards(): lax.all_to_all(picked, 'row', split_axis=0, concat_axis=0, tiled=True)  202 us
    dot_general x4, matrix products, coupled_tile(): jnp.dot(totals, package_cols, precision=lax.Precision.HIGHEST)  129 us
    gather x2, local copies, waits for them, and re-layouts, shards(): node_cond = via_mask.astype(jnp.float32) * jnp.take(bump_cond, bump_map)  45.5 us
    gather x2, local copies, waits for them, and re-layouts, shards(): supply_node = node_cond * jnp.take(bump_supply, bump_map)  45.5 us
    gather x2, local copies, waits for them, and re-layouts, shards(): picked = jnp.take(package, jnp.asarray(table, jnp.int32), axis=1)  37.4 us
    ppermute x8, starting transfers between devices, padded_2(): lax.ppermute(lax.slice_in_dim(block, block.shape[dim] - width, None, axis...  29.8 us
  transfers between devices with their start and end apart: 19, of which 3 were waited for; matrix products, arithmetic and copies ran while one was open for 19% of the time, Pallas kernels for 0%

commit v1 on v0

v1 whole, which is shorter than its diff:
```python
import collections
import functools

import jax
import jax.numpy as jnp
from jax import lax
from jax.experimental import pallas as pl
from jax.experimental.pallas import tpu as pltpu
from jax.sharding import PartitionSpec as P

BR = 128
BC = 64
DEG = 4

CHEB_LO = 0.05
CHEB_HI = 2.0
CHEB_MID = (CHEB_HI + CHEB_LO) / 2.0
CHEB_HALF = (CHEB_HI - CHEB_LO) / 2.0
CHEB_RATIO = CHEB_MID / CHEB_HALF

LANES = 128
SUBS = 8
AXES = ("row", "col")

Y_ROW = 0
PIECE_ROW = 2
SPILL_ROW = 4
HALO_ROW = 5
REL_ROW = 7
SECOND = 8

(LINK_R, LINK_L, LINK_D, LINK_U, VIA, WEIGHT, DIAG_T, DIAG_B, INV_T, INV_B) = range(10)

Geometry = collections.namedtuple(
    "Geometry",
    [
        "height",
        "breadth",
        "rows",
        "cols",
        "own",
        "block_rows",
        "block_cols",
        "tile_rows",
        "tile_cols",
        "lattice",
    ],
)


def steps_of():
    factors = [(0.0, 1.0 / CHEB_MID)]
    rho_now = 1.0 / CHEB_RATIO
    for _ in range(DEG - 1):
        rho_next = 1.0 / (2.0 * CHEB_RATIO - rho_now)
        factors.append((rho_next * rho_now, 2.0 * rho_next / CHEB_HALF))
        rho_now = rho_next
    return factors


def iota(shape, dim):
    return lax.broadcasted_iota(jnp.int32, shape, dim)


def lookup(table, index):
    return jnp.take_along_axis(table, index, axis=1, mode="promise_in_bounds")


def place():
    row = lax.axis_index("row")
    col = lax.axis_index("col")
    return row, col


def neighbours(geo, row, col):
    me = row * geo.cols + col
    east = jnp.where(col < geo.cols - 1, me + 1, me)
    west = jnp.where(col > 0, me - 1, me)
    south = jnp.where(row < geo.rows - 1, me + geo.cols, me)
    north = jnp.where(row > 0, me - geo.cols, me)
    return me, east, west, south, north


def per_band(geo):
    return geo.block_rows * BC // LANES


def spread(geo, ref, row, col, rel, tiles):
    span = per_band(geo)
    base = row * span
    count = geo.lattice // LANES
    lines = [ref[pl.ds(base + t, 1), :] for t in range(span)]
    lines.append(ref[pl.ds(jnp.minimum(base + span, count - 1), 1), :])
    per_line = LANES // BC
    sub = iota((SUBS, LANES), 0)
    lane = iota((SUBS, LANES), 1)
    last = geo.breadth // LANES
    columns = []
    for q in range(tiles):
        if q < last:
            columns.append(col * geo.block_cols + (lane + q * LANES) // geo.tile_cols)
        else:
            after = jnp.minimum((col + 1) * geo.block_cols, BC - 1)
            before = jnp.maximum(col * geo.block_cols - 1, 0)
            columns.append(jnp.where(lane < LANES // 2, after, before))
    bands = []
    for g in range(geo.height // SUBS):
        picks = []
        for shift in (0, 1):
            levels = [(g * SUBS + i) // geo.tile_rows + shift for i in range(SUBS)]
            held = [level // per_line for level in levels]
            table = jnp.broadcast_to(lines[held[0]], (SUBS, LANES))
            for i in range(1, SUBS):
                if held[i] != held[i - 1]:
                    table = jnp.where(
                        sub >= i, jnp.broadcast_to(lines[held[i]], (SUBS, LANES)), table
                    )
            part = ((g * SUBS + sub) // geo.tile_rows + shift) % per_line
            picks.append([lookup(table, part * BC + columns[q]) for q in range(tiles)])
        bands.append(
            jnp.concatenate(
                [
                    jnp.where(
                        rel[g * SUBS : (g + 1) * SUBS, q * LANES : (q + 1) * LANES] == 0,
                        picks[0][q],
                        picks[1][q],
                    )
                    for q in range(tiles)
                ],
                axis=1,
            )
        )
    return jnp.concatenate(bands, axis=0)


def shares(geo, weighted, rel, col):
    height, breadth = geo.height, geo.breadth
    near = jnp.where(rel == 0, weighted, 0.0)
    both = jnp.concatenate([near, weighted - near], axis=0)
    high = both.astype(jnp.bfloat16)
    rest = both - high.astype(jnp.float32)
    mid = rest.astype(jnp.bfloat16)
    low = (rest - mid.astype(jnp.float32)).astype(jnp.bfloat16)
    adder = (
        iota((breadth, LANES), 0) // geo.tile_cols == iota((breadth, LANES), 1) % geo.block_cols
    )
    adder = adder.astype(jnp.float32).astype(jnp.bfloat16)
    summed = jnp.dot(
        jnp.concatenate([high, mid, low], axis=0), adder, preferred_element_type=jnp.float32
    )
    summed = summed[: 2 * height] + summed[2 * height : 4 * height] + summed[4 * height :]
    sub = iota((SUBS, LANES), 0)
    segment = iota((SUBS, LANES), 1) // geo.block_cols
    segments = LANES // geo.block_cols
    packed = -(-geo.block_rows // segments)
    totals = [jnp.zeros((SUBS, LANES), jnp.float32) for _ in range(packed)]
    spill = jnp.zeros((SUBS, LANES), jnp.float32)
    for shift in (0, 1):
        for g in range(height // SUBS):
            first = g * SUBS // geo.tile_rows + shift
            final = (g * SUBS + SUBS - 1) // geo.tile_rows + shift
            level = (g * SUBS + sub) // geo.tile_rows + shift
            start = shift * height + g * SUBS
            block = summed[start : start + SUBS]
            for h in range(packed):
                if first < (h + 1) * segments and final >= h * segments:
                    hit = level == segment + h * segments
                    if final >= geo.block_rows:
                        hit = hit & (level < geo.block_rows)
                    totals[h] = totals[h] + jnp.where(hit, block, 0.0)
            if final >= geo.block_rows:
                hit = (level == geo.block_rows) & (segment == col)
                spill = spill + jnp.where(hit, block, 0.0)
    lines = [jnp.sum(total, axis=0, keepdims=True) for total in totals]
    return lines, jnp.sum(spill, axis=0, keepdims=True)


def gather_shares(geo, message, offset, out_ref):
    span = per_band(geo)
    per_line = LANES // BC
    segments = LANES // geo.block_cols
    sub = iota((SUBS, LANES), 0)
    lane = iota((SUBS, LANES), 1)
    level = sub * per_line + lane // BC
    index = (level % segments) * geo.block_cols + lane % geo.block_cols
    owner = (lane % BC) // geo.block_cols
    packed = -(-geo.block_rows // segments)

    def band(r):
        total = jnp.zeros((SUBS, LANES), jnp.float32)
        for c in range(geo.cols):
            sender = r * geo.cols + c
            table = jnp.broadcast_to(message[sender, pl.ds(offset + PIECE_ROW, 1), :], (SUBS, LANES))
            for h in range(1, packed):
                line = message[sender, pl.ds(offset + PIECE_ROW + h, 1), :]
                table = jnp.where(
                    sub >= h * segments // per_line, jnp.broadcast_to(line, (SUBS, LANES)), table
                )
            total = jnp.where(owner == c, lookup(table, index), total)
        return total

    def spill(r):
        line = message[r * geo.cols, pl.ds(offset + SPILL_ROW, 1), :]
        for c in range(1, geo.cols):
            line = line + message[r * geo.cols + c, pl.ds(offset + SPILL_ROW, 1), :]
        return jnp.where(sub == 0, jnp.broadcast_to(line, (SUBS, LANES)), 0.0)

    if geo.rows <= 8:
        for r in range(geo.rows):
            total = band(r)
            if r > 0:
                total = total + spill(r - 1)
            out_ref[pl.ds(r * span, span), :] = total[:span]
    else:

        def one(r, carry):
            above = jnp.where(r > 0, spill(jnp.maximum(r - 1, 0)), 0.0)
            out_ref[pl.ds(r * span, span), :] = (band(r) + above)[:span]
            return carry

        lax.fori_loop(0, geo.rows, one, 0)


def gather_own(geo, message, out_ref):
    devices = geo.rows * geo.cols
    if geo.own >= LANES:
        lines = geo.own // LANES
        for d in range(devices):
            out_ref[pl.ds(d * lines, lines), :] = message[d, Y_ROW : Y_ROW + lines, :]
    else:
        sharers = LANES // geo.own
        for t in range(devices // sharers):
            line = message[t * sharers, Y_ROW : Y_ROW + 1, :]
            for d in range(1, sharers):
                line = line + message[t * sharers + d, Y_ROW : Y_ROW + 1, :]
            out_ref[t : t + 1, :] = line


def product(geo, package_ref, sums_ref):
    groups = geo.own // SUBS
    totals = [jnp.zeros((SUBS, LANES), jnp.float32) for _ in range(groups)]
    for t in range(geo.lattice // LANES):
        line = jnp.broadcast_to(sums_ref[t : t + 1, :], (SUBS, LANES))
        for g in range(groups):
            block = package_ref[g * SUBS : (g + 1) * SUBS, t * LANES : (t + 1) * LANES]
            totals[g] = totals[g] + block * line
    return totals


def own_lines(geo, totals, start):
    per_line = min(len(totals), LANES // SUBS)
    sub = iota((SUBS, LANES), 0)
    lane = iota((SUBS, LANES), 1)
    lines = []
    for h in range(len(totals) // per_line):
        line = jnp.zeros((SUBS, LANES), jnp.float32)
        for q in range(per_line):
            column = jnp.sum(totals[h * per_line + q], axis=1, keepdims=True)
            line = jnp.where(lane == start + q * SUBS + sub, column, line)
        lines.append(jnp.sum(line, axis=0, keepdims=True))
    return lines


def own_start(geo, me):
    if geo.own >= LANES:
        return 0
    return (me % (LANES // geo.own)) * geo.own


def column_line(geo, field, at):
    sub = iota((SUBS, LANES), 0)
    lane = iota((SUBS, LANES), 1)
    total = jnp.zeros((SUBS, LANES), jnp.float32)
    for g in range(geo.height // SUBS):
        column = jnp.broadcast_to(field[g * SUBS : (g + 1) * SUBS, at : at + 1], (SUBS, LANES))
        total = total + jnp.where(lane == g * SUBS + sub, column, 0.0)
    return jnp.sum(total, axis=0, keepdims=True)


def line_column(geo, line):
    sub = iota((SUBS, LANES), 0)
    table = jnp.broadcast_to(line, (SUBS, LANES))
    return jnp.concatenate(
        [lookup(table, g * SUBS + sub) for g in range(geo.height // SUBS)], axis=0
    )


def beside(geo, field, east_line, west_line):
    lane = iota((geo.height, LANES), 1)
    extra = jnp.where(
        lane == 0,
        line_column(geo, east_line),
        jnp.where(lane == LANES - 1, line_column(geo, west_line), 0.0),
    )
    return jnp.concatenate([field, extra], axis=1)


def wide_lines(geo, line):
    return [line[:, q * LANES : (q + 1) * LANES] for q in range(geo.breadth // LANES)]


def wide_row(geo, message, sender, row=HALO_ROW):
    return jnp.concatenate(
        [message[sender, pl.ds(row + q, 1), :] for q in range(geo.breadth // LANES)], axis=1
    )


def tile_of(rows):
    empty = jnp.zeros((1, LANES), jnp.float32)
    return jnp.concatenate([rows.get(i, empty) for i in range(SUBS)], axis=0)


def put_all(ref, tile, offset=0):
    ref[:, offset : offset + SUBS, :] = jnp.broadcast_to(tile[None], (ref.shape[0],) + tile.shape)


def put(ref, target, row, lines):
    for i, line in enumerate(lines):
        ref[target, pl.ds(row + i, 1), :] = line


def share_rows(lines, spill):
    rows = {PIECE_ROW + i: line for i, line in enumerate(lines)}
    rows[SPILL_ROW] = spill
    return rows


def matrix(geo, state, top, low, top_wide, above, below):
    breadth = geo.breadth
    width = breadth + LANES
    after = pltpu.roll(top_wide, width - 1, 1)[:, :breadth]
    before = pltpu.roll(top_wide, 1, 1)[:, :breadth]
    row_at = iota((geo.height, breadth), 0)
    down = jnp.where(row_at == geo.height - 1, below, pltpu.roll(low, geo.height - 1, 0))
    up = jnp.where(row_at == 0, above, pltpu.roll(low, 1, 0))
    top_out = state(DIAG_T) * top - state(LINK_R) * after - state(LINK_L) * before - state(VIA) * low
    low_out = state(DIAG_B) * low - state(LINK_D) * down - state(LINK_U) * up - state(VIA) * top
    return top_out, low_out


def links(geo, row, col, wire_ref):
    height, breadth = geo.height, geo.breadth
    row_at = iota((height, breadth), 0)
    col_at = iota((height, breadth), 1)
    right = jnp.where((col == geo.cols - 1) & (col_at == breadth - 1), 0.0, wire_ref[0])
    down = jnp.where((row == geo.rows - 1) & (row_at == height - 1), 0.0, wire_ref[1])
    return right, down


def fetch(pairs, semaphores):
    copies = [
        pltpu.make_async_copy(source, target, semaphores.at[i])
        for i, (source, target) in enumerate(pairs)
    ]
    for copy in copies:
        copy.start()
    return copies


def open_kernel(geo, *refs):
    inputs, wave_ref, send, rel_ref = refs[:12], *refs[12:15]
    volt_ref, package_ref, decap_ref, decap_cond_ref, supply_ref, state_ref, source_ref = refs[15:22]
    map_ref, mask_ref, cond_ref, wire_ref, cap_ref, via_ref, load_ref, semaphores = refs[22:]
    early = (map_ref, mask_ref, cond_ref, volt_ref, wire_ref)
    late = (cap_ref, via_ref, load_ref, decap_ref, decap_cond_ref, supply_ref, package_ref)
    copies = fetch(tuple(zip(inputs, early + late)), semaphores)
    for copy in copies[: len(early)]:
        copy.wait()
    row, col = place()
    me, east, west, south, north = neighbours(geo, row, col)
    height, breadth = geo.height, geo.breadth
    own_level = row * geo.block_rows + iota((height, breadth), 0) // geo.tile_rows
    rel = lax.div(map_ref[...], jnp.int32(BC)) - own_level
    cond = spread(geo, cond_ref, row, col, rel, breadth // LANES)
    weight = mask_ref[...].astype(jnp.float32) * cond
    rel_ref[...] = rel
    top, low = volt_ref[0], volt_ref[1]
    right, down = links(geo, row, col, wire_ref)
    lines, spill = shares(geo, weight * top, rel, col)
    put_all(send, tile_of(share_rows(lines, spill)))
    put(send, east, HALO_ROW, [column_line(geo, top, breadth - 1), column_line(geo, right, breadth - 1)])
    put(send, west, HALO_ROW, [column_line(geo, top, 0)])
    put(send, north, HALO_ROW, wide_lines(geo, low[:1]))
    put(send, south, HALO_ROW, wide_lines(geo, low[height - 1 :]))
    put(send, south, Y_ROW, wide_lines(geo, down[height - 1 :]))
    for copy in copies[len(early) : -1]:
        copy.wait()
    via = via_ref[...]
    decap_cond = decap_cond_ref[...]
    frac = decap_cond / (1.0 + decap_cond)
    cap_top, cap_low = cap_ref[0], cap_ref[1]
    state_ref[LINK_R] = right
    state_ref[LINK_D] = down
    state_ref[VIA] = via
    state_ref[WEIGHT] = weight
    state_ref[DIAG_T] = cap_top + right + via + weight
    state_ref[DIAG_B] = cap_low + down + via + frac
    supply = spread(geo, supply_ref, row, col, rel, breadth // LANES)
    source_ref[0] = cap_top * top + weight * supply
    source_ref[1] = cap_low * low + frac * decap_ref[...] - wave_ref[0] * load_ref[...]
    copies[-1].wait()


def first_kernel(
    geo,
    message,
    package_ref,
    volt_ref,
    base_ref,
    source_ref,
    rel_ref,
    send,
    state_ref,
    residual_ref,
    direction_ref,
    sums_ref,
):
    row, col = place()
    me, east, west, south, north = neighbours(geo, row, col)
    height, breadth = geo.height, geo.breadth
    gather_shares(geo, message, 0, sums_ref)
    own = own_lines(geo, product(geo, package_ref, sums_ref), own_start(geo, me))

    rel = rel_ref[...]
    top, low = volt_ref[0], volt_ref[1]
    planes = {at: base_ref[at] for at in (LINK_R, LINK_D, VIA, WEIGHT)}
    weight, right, down = planes[WEIGHT], planes[LINK_R], planes[LINK_D]
    row_at = iota((height, breadth), 0)
    first_col = iota((height, LANES), 1) == 0
    edge = jnp.where(col > 0, message[west, HALO_ROW + 1 : HALO_ROW + 2, :], 0.0)
    left = pltpu.roll(right, 1, 1)
    left = jnp.concatenate(
        [jnp.where(first_col, line_column(geo, edge), left[:, :LANES]), left[:, LANES:]], axis=1
    )
    edge = jnp.where(row > 0, wide_row(geo, message, north, Y_ROW), 0.0)
    up = jnp.where(row_at == 0, edge, pltpu.roll(down, 1, 0))
    diag_top = base_ref[DIAG_T] + left
    diag_low = base_ref[DIAG_B] + up
    planes.update(
        {
            LINK_L: left,
            LINK_U: up,
            DIAG_T: diag_top,
            DIAG_B: diag_low,
            INV_T: 1.0 / diag_top,
            INV_B: 1.0 / diag_low,
        }
    )
    for at, plane in planes.items():
        state_ref[at] = plane
    wide = beside(
        geo,
        top,
        message[east, HALO_ROW : HALO_ROW + 1, :],
        message[west, HALO_ROW : HALO_ROW + 1, :],
    )
    top_out, low_out = matrix(
        geo,
        planes.__getitem__,
        top,
        low,
        wide,
        wide_row(geo, message, north),
        wide_row(geo, message, south),
    )
    residual_top = source_ref[0] - top_out
    residual_low = source_ref[1] - low_out
    residual_ref[0] = residual_top
    residual_ref[1] = residual_low
    gain = steps_of()[0][1]
    direction_top = gain * residual_top * planes[INV_T]
    direction_low = gain * residual_low * planes[INV_B]
    direction_ref[0] = direction_top
    direction_ref[1] = direction_low
    pull = weight * planes[INV_T]
    lines, spill = shares(geo, weight * direction_top, rel, col)
    rows = share_rows(lines, spill)
    rows.update({Y_ROW + i: line for i, line in enumerate(own)})
    put_all(send, tile_of(rows))
    lines, spill = shares(geo, weight * pull, rel, col)
    put_all(send, tile_of(share_rows(lines, spill)), SECOND)
    below = rel.astype(jnp.float32)
    for target, at in ((east, breadth - 1), (west, 0)):
        fields = (direction_top, pull, below)
        put(send, target, HALO_ROW, [column_line(geo, field, at) for field in fields])
    put(send, north, HALO_ROW, wide_lines(geo, direction_low[:1]))
    put(send, south, HALO_ROW, wide_lines(geo, direction_low[height - 1 :]))


def finish_direction(geo, message, product_ref, row, col, stage, direction, pull, rel):
    gain = steps_of()[stage][1]
    coupled = spread(geo, product_ref, row, col, rel, rel.shape[1] // LANES)
    return direction + gain * pull * coupled, coupled


def step_kernel(geo, stage, *refs):
    if stage == 1:
        (message, package_ref, state_ref, residual_in, direction_in, iterate_in, rel_ref) = refs[:7]
        (send, residual_ref, direction_ref, iterate_ref, pull_ref, wide_rel_ref, squares_ref) = refs[7:14]
    else:
        (message, package_ref, state_ref, residual_in, direction_in, iterate_in) = refs[:6]
        (pull_ref, wide_rel_ref, squares_ref) = refs[6:9]
        (send, iterate_ref) = refs[9:11]
        if stage < DEG - 1:
            (residual_ref, direction_ref) = refs[11:13]
    product_ref, sums_ref = refs[-2:]
    row, col = place()
    me, east, west, south, north = neighbours(geo, row, col)
    height, breadth = geo.height, geo.breadth
    gain_before = steps_of()[stage - 1][1]
    gather_own(geo, message, product_ref)
    gather_shares(geo, message, 0, sums_ref)
    if stage == 1:
        gather_shares(geo, message, SECOND, squares_ref)
    sums_ref[...] = sums_ref[...] + gain_before * squares_ref[...] * product_ref[...]
    own = own_lines(geo, product(geo, package_ref, sums_ref), own_start(geo, me))

    def state(at):
        return state_ref[at]

    weight = state(WEIGHT)
    if stage == 1:
        pull = beside(
            geo,
            weight * state(INV_T),
            message[east, HALO_ROW + 1 : HALO_ROW + 2, :],
            message[west, HALO_ROW + 1 : HALO_ROW + 2, :],
        )
        wide_rel = beside(
            geo,
            rel_ref[...].astype(jnp.float32),
            message[east, REL_ROW : REL_ROW + 1, :],
            message[west, REL_ROW : REL_ROW + 1, :],
        ).astype(jnp.int32)
        pull_ref[...] = pull
        wide_rel_ref[...] = wide_rel
    else:
        pull = pull_ref[...]
        wide_rel = wide_rel_ref[...]
    rel = wide_rel[:, :breadth]
    wide = beside(
        geo,
        direction_in[0],
        message[east, HALO_ROW : HALO_ROW + 1, :],
        message[west, HALO_ROW : HALO_ROW + 1, :],
    )
    wide, coupled = finish_direction(
        geo, message, product_ref, row, col, stage - 1, wide, pull, wide_rel
    )
    top = wide[:, :breadth]
    low = direction_in[1]
    top_out, low_out = matrix(
        geo,
        state,
        top,
        low,
        wide,
        wide_row(geo, message, north),
        wide_row(geo, message, south),
    )
    residual_top = residual_in[0] + weight * coupled[:, :breadth] - top_out
    residual_low = residual_in[1] - low_out
    keep, gain = steps_of()[stage]
    direction_top = keep * top + gain * residual_top * state(INV_T)
    direction_low = keep * low + gain * residual_low * state(INV_B)
    iterate_top = iterate_in[0] + top
    iterate_low = iterate_in[1] + low
    if stage == DEG - 1:
        iterate_top = iterate_top + direction_top
        iterate_low = iterate_low + direction_low
        lines, spill = shares(geo, weight * iterate_top, rel, col)
    else:
        residual_ref[0] = residual_top
        residual_ref[1] = residual_low
        direction_ref[0] = direction_top
        direction_ref[1] = direction_low
        lines, spill = shares(geo, weight * direction_top, rel, col)
    iterate_ref[0] = iterate_top
    iterate_ref[1] = iterate_low
    rows = share_rows(lines, spill)
    rows.update({Y_ROW + i: line for i, line in enumerate(own)})
    put_all(send, tile_of(rows))
    if stage < DEG - 1:
        put(send, east, HALO_ROW, [column_line(geo, direction_top, breadth - 1)])
        put(send, west, HALO_ROW, [column_line(geo, direction_top, 0)])
        put(send, north, HALO_ROW, wide_lines(geo, direction_low[:1]))
        put(send, south, HALO_ROW, wide_lines(geo, direction_low[height - 1 :]))


def last_kernel(
    geo,
    message,
    package_ref,
    iterate_ref,
    pull_ref,
    wide_rel_ref,
    squares_ref,
    decap_ref,
    decap_cond_ref,
    supply_ref,
    voltage_ref,
    decap_volt_ref,
    bump_volt_ref,
    product_ref,
    sums_ref,
):
    row, col = place()
    me = row * geo.cols + col
    breadth = geo.breadth
    gain = steps_of()[DEG - 1][1]
    gather_own(geo, message, product_ref)
    gather_shares(geo, message, 0, sums_ref)
    sums_ref[...] = sums_ref[...] + gain * squares_ref[...] * product_ref[...]
    own = own_lines(geo, product(geo, package_ref, sums_ref), 0)
    if geo.own >= LANES:
        supply = supply_ref[pl.ds(me * len(own), len(own)), :]
        bump_volt_ref[...] = supply + jnp.concatenate(own, axis=0)
    else:
        sharers = LANES // geo.own
        line = jnp.broadcast_to(supply_ref[pl.ds(me // sharers, 1), :], (SUBS, LANES))
        line = lookup(line, (iota((SUBS, LANES), 1) + own_start(geo, me)) % LANES)
        bump_volt_ref[...] = (line[:1] + own[0])[:, : geo.own]
    coupled = spread(
        geo, product_ref, row, col, wide_rel_ref[:, :breadth], breadth // LANES
    )
    low = iterate_ref[1]
    voltage_ref[0] = iterate_ref[0] + gain * pull_ref[:, :breadth] * coupled
    voltage_ref[1] = low
    decap_cond = decap_cond_ref[...]
    decap_volt_ref[...] = (decap_ref[...] + decap_cond * low) / (1.0 + decap_cond)


def exchange(message):
    return lax.all_to_all(message, AXES, split_axis=0, concat_axis=0, tiled=True)


def call(kernel, operands, outputs, scratch=(), outside=(), scalar=None):
    inside = pl.BlockSpec(memory_space=pltpu.VMEM)
    specs = [inside] * len(operands)
    if scalar is not None:
        specs[scalar] = pl.BlockSpec(memory_space=pltpu.SMEM)
    specs = [pl.BlockSpec(memory_space=pltpu.HBM)] * len(outside) + specs
    outside = [pltpu.with_memory_space_constraint(array, pltpu.HBM) for array in outside]
    out_specs = [
        pl.BlockSpec(memory_space=getattr(output, "memory_space", pltpu.VMEM)) for output in outputs
    ]
    return pl.pallas_call(
        kernel,
        out_shape=list(outputs),
        in_specs=specs,
        out_specs=out_specs,
        scratch_shapes=list(scratch),
        compiler_params=pltpu.CompilerParams(vmem_limit_bytes=16 * 2**20),
    )(*outside, *operands)


def shards(
    volt_start,
    cap_dt,
    wire_cond,
    via_cond,
    load_current,
    load_wave,
    decap_state,
    decap_cond,
    bump_map,
    via_mask,
    bump_cond,
    bump_supply,
    package,
):
    height, breadth = via_cond.shape
    rows, cols = lax.axis_size("row"), lax.axis_size("col")
    block_rows, block_cols = BR // rows, BC // cols
    own, lattice = package.shape
    geo = Geometry(
        height,
        breadth,
        rows,
        cols,
        own,
        block_rows,
        block_cols,
        height // block_rows,
        breadth // block_cols,
        lattice,
    )
    devices = rows * cols
    f32 = jnp.float32
    table = (lattice // LANES, LANES)
    cond = bump_cond.reshape(table)
    supply = bump_supply.reshape(table)
    field = pltpu.VMEM((height, breadth), f32)
    pair = pltpu.VMEM((2, height, breadth), f32)
    message = pltpu.VMEM((devices, SUBS, LANES), f32)
    held = pltpu.VMEM(table, f32)

    whole = pltpu.VMEM((height, breadth), jnp.int32)
    sent, rel, volt, package, decap, decap_cond, supply, base, source = call(
        functools.partial(open_kernel, geo),
        (load_wave,),
        (
            message,
            whole,
            pair,
            pltpu.VMEM(package.shape, f32),
            field,
            field,
            held,
            pltpu.VMEM((10, height, breadth), f32),
            pair,
        ),
        (whole, whole, held, pair, pair, field, field, pltpu.SemaphoreType.DMA((12,))),
        outside=(
            bump_map,
            via_mask,
            cond,
            volt_start,
            wire_cond,
            cap_dt,
            via_cond,
            load_current,
            decap_state,
            decap_cond,
            supply,
            package,
        ),
        scalar=0,
    )
    sent, state, residual, direction = call(
        functools.partial(first_kernel, geo),
        (exchange(sent), package, volt, base, source, rel),
        (
            pltpu.VMEM((devices, 2 * SUBS, LANES), f32),
            pltpu.VMEM((10, height, breadth), f32),
            pair,
            pair,
        ),
        (held,),
    )
    wide = (height, breadth + LANES)
    sent, residual, direction, iterate, pull, wide_rel, squares = call(
        functools.partial(step_kernel, geo, 1),
        (exchange(sent), package, state, residual, direction, volt, rel),
        (message, pair, pair, pair, pltpu.VMEM(wide, f32), pltpu.VMEM(wide, jnp.int32), held),
        (held, held),
    )
    for stage in range(2, DEG):
        sent, iterate, *carried = call(
            functools.partial(step_kernel, geo, stage),
            (
                exchange(sent),
                package,
                state,
                residual,
                direction,
                iterate,
                pull,
                wide_rel,
                squares,
            ),
            (message, pair, pair, pair) if stage < DEG - 1 else (message, pair),
            (held, held),
        )
        if carried:
            residual, direction = carried
    voltage, decap_volt, bump_volt = call(
        functools.partial(last_kernel, geo),
        (
            exchange(sent),
            package,
            iterate,
            pull,
            wide_rel,
            squares,
            decap,
            decap_cond,
            supply,
        ),
        (
            jax.ShapeDtypeStruct((2, height, breadth), f32),
            jax.ShapeDtypeStruct((height, breadth), f32),
            jax.ShapeDtypeStruct((max(1, own // LANES), min(own, LANES)), f32),
        ),
        (held, held),
    )
    return voltage, decap_volt, bump_volt.reshape(own)


def solution(mesh):
    field = P("row", "col")
    pair = P(None, "row", "col")
    return jax.shard_map(
        shards,
        mesh=mesh,
        in_specs=(
            pair,
            pair,
            pair,
            field,
            field,
            P(),
            field,
            field,
            field,
            field,
            P(),
            P(),
            P(AXES, None),
        ),
        out_specs=(pair, field, P(AXES)),
        check_vma=False,
    )
```

time: 825 us -> 69.5 us (0.08)
  blocking collectives: 410 us -> 58.2 us
  local copies, waits for them, and re-layouts: 190 us -> 0 us
  matrix products: 138 us -> 0 us
  starting transfers between devices: 51.4 us -> 0 us
  other arithmetic: 13.4 us -> 0 us
  waiting for transfers between devices: 12.3 us -> 0 us
  Pallas kernels: 0 us -> 9.74 us
    psum x5 -> x0, blocking collectives: 208 us -> none  [bump_totals(): return lax.psum(canvas[:BR].reshape(-1), ('row', 'col'))]
    all_to_all x1 -> x5, blocking collectives: 202 us -> 58.2 us  [exchange(): lax.all_to_all(message, AXES, split_axis=0, concat_axis=0, tiled=True)]
    dot_general x5 -> x0, matrix products: 138 us -> none  [the longest x4 129 us: coupled_tile(): jnp.dot(totals, package_cols, precision=lax.Precision.HIGHEST)]
    gather x10 -> x0, local copies, waits for them, and re-layouts: 132 us -> none  [the longest x2 45.5 us: shards(): node_cond = via_mask.astype(jnp.float32) * jnp.take(bump_cond, bump_map)]
    ppermute x18 -> x0, starting transfers between devices: 45.5 us -> none  [the longest x8 29.8 us: padded_2(): lax.ppermute(lax.slice_in_dim(block, block.shape[dim] - width, None, axis...]
    all_to_all x2 -> x0, local copies, waits for them, and re-layouts: 21.4 us -> none  [the longest x1 12.7 us: shards(): lax.all_to_all(lax.all_to_all(picked, 'row', split_axis=0, concat_axis=0,...]
    ppermute x18 -> x0, waiting for transfers between devices: 12.3 us -> none  [the longest x8 12.3 us: padded_2(): lax.ppermute(lax.slice_in_dim(block, 0, width, axis=dim), axis, backward)]
    reshape x6 -> x0, local copies, waits for them, and re-layouts: 12.1 us -> none  [the longest x1 11.7 us: shards(): package_cols = moved.reshape(bump_count, win_rows * win_cols)]
  transfers between devices with their start and end apart: 19 -> 0, of which waited for: 3 -> 0; matrix products, arithmetic and copies ran while one was open for 19% -> 0% of each run, Pallas kernels for 0% -> 0%
where the time goes in v1:
time: 69.5 us; the launch traced here: 69.2 us
  blocking collectives  58.2 us (84%)
  Pallas kernels  9.74 us (14%)
  between operations  1.32 us (2%)
    all_to_all x5, blocking collectives, exchange(): lax.all_to_all(message, AXES, split_axis=0, concat_axis=0, tiled=True)  58.2 us
    pallas_call x6, Pallas kernels, call(): pl.pallas_call(kernel, out_shape=list(outputs), in_specs=specs, out_specs...  9.74 us

profile of v1, /device:TPU:0, one launch (start us, length us, event | category | flops | bytes accessed | tf_op | source)
XLA Modules:
  0.0 69.2 jit_solution(4615086714932754636)
XLA Ops:
  1.3 3.8 %shard_map.148 = (f32[32,8,128]{2,1,0:T(8,128)S(1)}, s32[32,256]{1,0:T(8,128)S(1)}, f32[2,32,256]{2,1,0:T(8,128)S(1)}, f32[256,8192]{1,0:T(8,128)S(1)}, f32[32,2...) custom-call(s32[32,256]{1,0:T(8,128)} %refs_0_.1, ...), custom_call_target="tpu_custom_call" | custom-call | tf_op jit(solution)/shard_map/pallas_call | solution.py:647
  5.1 15.3 %all_to_all.25.message = f32[32,8,128]{2,1,0:T(8,128)S(1)} all-to-all(f32[32,8,128]{2,1,0:T(8,128)S(1)} %get-tuple-element.32), channel_id=1, replica_groups=mesh['row'=8,'col'=4] {'row','col'}, dimensions={0} | all-to-all | bytes 262144 | tf_op jit(solution)/shard_map/all_to_all | solution.py:634
  20.4 1.1 %shard_map.149 = (f32[32,16,128]{2,1,0:T(8,128)S(1)}, f32[10,32,256]{2,1,0:T(8,128)S(1)}, f32[2,32,256]{2,1,0:T(8,128)S(1)}, f32[2,32,256]{2,1,0:T(8,128)S(1)}) custom-call(f32[32,8,128]{2,1,0:T(8,128)S(1)} %all_to_all.25.message, f32[256,8192]{1,0:T(8,128)S(1)} %get-tuple-element.33.package_ref.refs_1_, ...), custom_call_target="tpu_custom_call" | custom-call | tf_op jit(solution)/shard_map/pallas_call | solution.py:647
  21.5 12.4 %all_to_all.26.refs_0_ = f32[32,16,128]{2,1,0:T(8,128)S(1)} all-to-all(f32[32,16,128]{2,1,0:T(8,128)S(1)} %get-tuple-element.38), channel_id=1, replica_groups=mesh['row'=8,'col'=4] {'row','col'}, dimensions={0} | all-to-all | bytes 524288 | tf_op jit(solution)/shard_map/all_to_all | solution.py:634
  33.8 1.0 %shard_map.150 = (f32[32,8,128]{2,1,0:T(8,128)S(1)}, f32[2,32,256]{2,1,0:T(8,128)S(1)}, f32[2,32,256]{2,1,0:T(8,128)S(1)}, f32[2,32,256]{2,1,0:T(8,128)S(1)}, f3...) custom-call(f32[32,16,128]{2,1,0:T(8,128)S(1)} %all_to_all.26.refs_0_, ...), custom_call_target="tpu_custom_call" | custom-call | tf_op jit(solution)/shard_map/pallas_call | solution.py:647
  34.9 10.4 %all_to_all.27.refs_0_ = f32[32,8,128]{2,1,0:T(8,128)S(1)} all-to-all(f32[32,8,128]{2,1,0:T(8,128)S(1)} %get-tuple-element.42), channel_id=1, replica_groups=mesh['row'=8,'col'=4] {'row','col'}, dimensions={0} | all-to-all | bytes 262144 | tf_op jit(solution)/shard_map/all_to_all | solution.py:634
  45.3 1.2 %shard_map.151 = (f32[32,8,128]{2,1,0:T(8,128)S(1)}, f32[2,32,256]{2,1,0:T(8,128)S(1)}, f32[2,32,256]{2,1,0:T(8,128)S(1)}, f32[2,32,256]{2,1,0:T(8,128)S(1)}) custom-call(f32[32,8,128]{2,1,0:T(8,128)S(1)} %all_to_all.27.refs_0_, f32[256,8192]{1,0:T(8,128)S(1)} %get-tuple-element.33.package_ref.refs_1_, f32[10,32,256]{2,1,0:T(8,128)S(1)} %get-tuple-element.39.refs_2_, ...), custom_call_target="tpu_custom_call" | custom-call | tf_op jit(solution)/shard_map/pallas_call | solution.py:647
  46.5 10.0 %all_to_all.28.refs_0_ = f32[32,8,128]{2,1,0:T(8,128)S(1)} all-to-all(f32[32,8,128]{2,1,0:T(8,128)S(1)} %get-tuple-element.49), channel_id=1, replica_groups=mesh['row'=8,'col'=4] {'row','col'}, dimensions={0} | all-to-all | bytes 262144 | tf_op jit(solution)/shard_map/all_to_all | solution.py:634
  56.5 1.1 %shard_map.152 = (f32[32,8,128]{2,1,0:T(8,128)S(1)}, f32[2,32,256]{2,1,0:T(8,128)S(1)}) custom-call(f32[32,8,128]{2,1,0:T(8,128)S(1)} %all_to_all.28.refs_0_, f32[256,8192]{1,0:T(8,128)S(1)} %get-tuple-element.33.package_ref.refs_1_, f32[10,32,256]{2,1,0:T(8,128)S(1)} %get-tuple-element.39.refs_2_, f32[2,32,256]{2,1,0:T(8,128)S(1)} %get-tuple-element.50.refs_3_, ...), custom_call_target="tpu_custom_call" | custom-call | tf_op jit(solution)/shard_map/pallas_call | solution.py:647
  57.6 10.0 %all_to_all.29.message = f32[32,8,128]{2,1,0:T(8,128)S(1)} all-to-all(f32[32,8,128]{2,1,0:T(8,128)S(1)} %get-tuple-element.53), channel_id=1, replica_groups=mesh['row'=8,'col'=4] {'row','col'}, dimensions={0} | all-to-all | bytes 262144 | tf_op jit(solution)/shard_map/all_to_all | solution.py:634
  67.6 1.6 %shard_map.153 = (f32[2,32,256]{2,1,0:T(8,128)}, f32[32,256]{1,0:T(8,128)}, f32[2,128]{1,0:T(2,128)}) custom-call(f32[32,8,128]{2,1,0:T(8,128)S(1)} %all_to_all.29.message, f32[256,8192]{1,0:T(8,128)S(1)} %get-tuple-element.33.package_ref.refs_1_, f32[2,32,256]{2,1,0:T(8,128)S(1)} %get-tuple-element.54.iterate_ref, ...), custom_call_target="tpu_custom_call" | custom-call | tf_op jit(solution)/shard_map/pallas_call | solution.py:647

commit v2 on v1

--- a/solution.py
+++ b/solution.py
@@ -22,12 +22,10 @@
 SUBS = 8
 AXES = ("row", "col")
 
-Y_ROW = 0
-PIECE_ROW = 2
-SPILL_ROW = 4
-HALO_ROW = 5
-REL_ROW = 7
-SECOND = 8
+FIRST = ("share", "spill", "halo", "deep")
+SECOND = ("own", "share", "spill", "square", "halo")
+NEXT = ("own", "share", "spill", "halo")
+LAST = ("own", "share", "spill")
 
 (LINK_R, LINK_L, LINK_D, LINK_U, VIA, WEIGHT, DIAG_T, DIAG_B, INV_T, INV_B) = range(10)
 
@@ -46,6 +44,27 @@
         "lattice",
     ],
 )
+
+
+def rows_of(geo, parts):
+    sizes = {
+        "own": max(1, geo.own // LANES),
+        "share": -(-geo.block_rows * geo.block_cols // LANES),
+        "square": -(-geo.block_rows * geo.block_cols // LANES),
+        "spill": 1,
+        "halo": geo.breadth // LANES,
+        "deep": geo.breadth // LANES,
+    }
+    starts, end = {}, 0
+    for part in parts:
+        starts[part] = end
+        end += sizes[part]
+    starts["end"] = end
+    return starts
+
+
+def row_at(message, device, row):
+    return message[device, :, row * LANES : (row + 1) * LANES]
 
 
 def steps_of():
@@ -133,7 +152,7 @@
     return jnp.concatenate(bands, axis=0)
 
 
-def shares(geo, weighted, rel, col):
+def shares(geo, weighted, rel, col, half=0):
     height, breadth = geo.height, geo.breadth
     near = jnp.where(rel == 0, weighted, 0.0)
     both = jnp.concatenate([near, weighted - near], axis=0)
@@ -153,6 +172,7 @@
     segment = iota((SUBS, LANES), 1) // geo.block_cols
     segments = LANES // geo.block_cols
     packed = -(-geo.block_rows // segments)
+    slot = col + half * (BC // geo.block_cols)
     totals = [jnp.zeros((SUBS, LANES), jnp.float32) for _ in range(packed)]
     spill = jnp.zeros((SUBS, LANES), jnp.float32)
     for shift in (0, 1):
@@ -169,13 +189,13 @@
                         hit = hit & (level < geo.block_rows)
                     totals[h] = totals[h] + jnp.where(hit, block, 0.0)
             if final >= geo.block_rows:
-                hit = (level == geo.block_rows) & (segment == col)
+                hit = (level == geo.block_rows) & (segment == slot)
                 spill = spill + jnp.where(hit, block, 0.0)
     lines = [jnp.sum(total, axis=0, keepdims=True) for total in totals]
     return lines, jnp.sum(spill, axis=0, keepdims=True)
 
 
-def gather_shares(geo, message, offset, out_ref):
+def gather_shares(geo, message, starts, out_ref, part="share", half=0):
     span = per_band(geo)
     per_line = LANES // BC
     segments = LANES // geo.block_cols
@@ -190,9 +210,9 @@
         total = jnp.zeros((SUBS, LANES), jnp.float32)
         for c in range(geo.cols):
             sender = r * geo.cols + c
-            table = jnp.broadcast_to(message[sender, pl.ds(offset + PIECE_ROW, 1), :], (SUBS, LANES))
+            table = jnp.broadcast_to(row_at(message, sender, starts[part]), (SUBS, LANES))
             for h in range(1, packed):
-                line = message[sender, pl.ds(offset + PIECE_ROW + h, 1), :]
+                line = row_at(message, sender, starts[part] + h)
                 table = jnp.where(
                     sub >= h * segments // per_line, jnp.broadcast_to(line, (SUBS, LANES)), table
                 )
@@ -200,10 +220,13 @@
         return total
 
     def spill(r):
-        line = message[r * geo.cols, pl.ds(offset + SPILL_ROW, 1), :]
+        line = row_at(message, r * geo.cols, starts["spill"])
         for c in range(1, geo.cols):
-            line = line + message[r * geo.cols + c, pl.ds(offset + SPILL_ROW, 1), :]
-        return jnp.where(sub == 0, jnp.broadcast_to(line, (SUBS, LANES)), 0.0)
+            line = line + row_at(message, r * geo.cols + c, starts["spill"])
+        line = jnp.broadcast_to(line, (SUBS, LANES))
+        if half:
+            line = pltpu.roll(line, LANES - half * BC, 1)
+        return jnp.where((sub == 0) & (lane < BC), line, 0.0)
 
     if geo.rows <= 8:
         for r in range(geo.rows):
@@ -221,18 +244,20 @@
         lax.fori_loop(0, geo.rows, one, 0)
 
 
-def gather_own(geo, message, out_ref):
+def gather_own(geo, message, starts, out_ref):
     devices = geo.rows * geo.cols
     if geo.own >= LANES:
         lines = geo.own // LANES
         for d in range(devices):
-            out_ref[pl.ds(d * lines, lines), :] = message[d, Y_ROW : Y_ROW + lines, :]
+            for i in range(lines):
+                at = d * lines + i
+                out_ref[at : at + 1, :] = row_at(message, d, starts["own"] + i)
     else:
         sharers = LANES // geo.own
         for t in range(devices // sharers):
-            line = message[t * sharers, Y_ROW : Y_ROW + 1, :]
+            line = row_at(message, t * sharers, starts["own"])
             for d in range(1, sharers):
-                line = line + message[t * sharers + d, Y_ROW : Y_ROW + 1, :]
+                line = line + row_at(message, t * sharers + d, starts["own"])
             out_ref[t : t + 1, :] = line
 
 
@@ -267,30 +292,30 @@
     return (me % (LANES // geo.own)) * geo.own
 
 
-def column_line(geo, field, at):
+def column_line(geo, field, at, start=0):
     sub = iota((SUBS, LANES), 0)
     lane = iota((SUBS, LANES), 1)
     total = jnp.zeros((SUBS, LANES), jnp.float32)
     for g in range(geo.height // SUBS):
         column = jnp.broadcast_to(field[g * SUBS : (g + 1) * SUBS, at : at + 1], (SUBS, LANES))
-        total = total + jnp.where(lane == g * SUBS + sub, column, 0.0)
+        total = total + jnp.where(lane == start + g * SUBS + sub, column, 0.0)
     return jnp.sum(total, axis=0, keepdims=True)
 
 
-def line_column(geo, line):
+def line_column(geo, line, start=0):
     sub = iota((SUBS, LANES), 0)
     table = jnp.broadcast_to(line, (SUBS, LANES))
     return jnp.concatenate(
-        [lookup(table, g * SUBS + sub) for g in range(geo.height // SUBS)], axis=0
-    )
-
-
-def beside(geo, field, east_line, west_line):
+        [lookup(table, start + g * SUBS + sub) for g in range(geo.height // SUBS)], axis=0
+    )
+
+
+def beside(geo, field, east_line, west_line, start=0):
     lane = iota((geo.height, LANES), 1)
     extra = jnp.where(
         lane == 0,
-        line_column(geo, east_line),
-        jnp.where(lane == LANES - 1, line_column(geo, west_line), 0.0),
+        line_column(geo, east_line, start),
+        jnp.where(lane == LANES - 1, line_column(geo, west_line, start), 0.0),
     )
     return jnp.concatenate([field, extra], axis=1)
 
@@ -299,30 +324,26 @@
     return [line[:, q * LANES : (q + 1) * LANES] for q in range(geo.breadth // LANES)]
 
 
-def wide_row(geo, message, sender, row=HALO_ROW):
+def wide_row(geo, message, sender, row):
     return jnp.concatenate(
-        [message[sender, pl.ds(row + q, 1), :] for q in range(geo.breadth // LANES)], axis=1
-    )
-
-
-def tile_of(rows):
-    empty = jnp.zeros((1, LANES), jnp.float32)
-    return jnp.concatenate([rows.get(i, empty) for i in range(SUBS)], axis=0)
-
-
-def put_all(ref, tile, offset=0):
-    ref[:, offset : offset + SUBS, :] = jnp.broadcast_to(tile[None], (ref.shape[0],) + tile.shape)
+        [row_at(message, sender, row + q) for q in range(geo.breadth // LANES)], axis=1
+    )
+
+
+def put_all(ref, row, lines):
+    for i, line in enumerate(lines):
+        to = (row + i) * LANES
+        ref[:, :, to : to + LANES] = jnp.broadcast_to(line[None], (ref.shape[0], 1, LANES))
 
 
 def put(ref, target, row, lines):
     for i, line in enumerate(lines):
-        ref[target, pl.ds(row + i, 1), :] = line
-
-
-def share_rows(lines, spill):
-    rows = {PIECE_ROW + i: line for i, line in enumerate(lines)}
-    rows[SPILL_ROW] = spill
-    return rows
+        to = (row + i) * LANES
+        ref[target, :, to : to + LANES] = line
+
+
+def blank(geo):
+    return [jnp.zeros((1, LANES), jnp.float32)] * (geo.breadth // LANES)
 
 
 def matrix(geo, state, top, low, top_wide, above, below):
@@ -330,9 +351,9 @@
     width = breadth + LANES
     after = pltpu.roll(top_wide, width - 1, 1)[:, :breadth]
     before = pltpu.roll(top_wide, 1, 1)[:, :breadth]
-    row_at = iota((geo.height, breadth), 0)
-    down = jnp.where(row_at == geo.height - 1, below, pltpu.roll(low, geo.height - 1, 0))
-    up = jnp.where(row_at == 0, above, pltpu.roll(low, 1, 0))
+    line_at = iota((geo.height, breadth), 0)
+    down = jnp.where(line_at == geo.height - 1, below, pltpu.roll(low, geo.height - 1, 0))
+    up = jnp.where(line_at == 0, above, pltpu.roll(low, 1, 0))
     top_out = state(DIAG_T) * top - state(LINK_R) * after - state(LINK_L) * before - state(VIA) * low
     low_out = state(DIAG_B) * low - state(LINK_D) * down - state(LINK_U) * up - state(VIA) * top
     return top_out, low_out
@@ -340,10 +361,10 @@
 
 def links(geo, row, col, wire_ref):
     height, breadth = geo.height, geo.breadth
-    row_at = iota((height, breadth), 0)
+    line_at = iota((height, breadth), 0)
     col_at = iota((height, breadth), 1)
     right = jnp.where((col == geo.cols - 1) & (col_at == breadth - 1), 0.0, wire_ref[0])
-    down = jnp.where((row == geo.rows - 1) & (row_at == height - 1), 0.0, wire_ref[1])
+    down = jnp.where((row == geo.rows - 1) & (line_at == height - 1), 0.0, wire_ref[1])
     return right, down
 
 
@@ -377,12 +398,15 @@
     top, low = volt_ref[0], volt_ref[1]
     right, down = links(geo, row, col, wire_ref)
     lines, spill = shares(geo, weight * top, rel, col)
-    put_all(send, tile_of(share_rows(lines, spill)))
-    put(send, east, HALO_ROW, [column_line(geo, top, breadth - 1), column_line(geo, right, breadth - 1)])
-    put(send, west, HALO_ROW, [column_line(geo, top, 0)])
-    put(send, north, HALO_ROW, wide_lines(geo, low[:1]))
-    put(send, south, HALO_ROW, wide_lines(geo, low[height - 1 :]))
-    put(send, south, Y_ROW, wide_lines(geo, down[height - 1 :]))
+    starts = rows_of(geo, FIRST)
+    halo = starts["halo"]
+    put_all(send, starts["share"], lines + [spill])
+    put(send, me, halo, blank(geo))
+    put(send, east, halo, [column_line(geo, top, breadth - 1), column_line(geo, right, breadth - 1)])
+    put(send, west, halo, [column_line(geo, top, 0)])
+    put(send, north, halo, wide_lines(geo, low[:1]))
+    put(send, south, halo, wide_lines(geo, low[height - 1 :]))
+    put(send, south, starts["deep"], wide_lines(geo, down[height - 1 :]))
     for copy in copies[len(early) : -1]:
         copy.wait()
     via = via_ref[...]
@@ -418,22 +442,24 @@
     row, col = place()
     me, east, west, south, north = neighbours(geo, row, col)
     height, breadth = geo.height, geo.breadth
-    gather_shares(geo, message, 0, sums_ref)
+    starts = rows_of(geo, FIRST)
+    halo = starts["halo"]
+    gather_shares(geo, message, starts, sums_ref)
     own = own_lines(geo, product(geo, package_ref, sums_ref), own_start(geo, me))
 
     rel = rel_ref[...]
     top, low = volt_ref[0], volt_ref[1]
     planes = {at: base_ref[at] for at in (LINK_R, LINK_D, VIA, WEIGHT)}
     weight, right, down = planes[WEIGHT], planes[LINK_R], planes[LINK_D]
-    row_at = iota((height, breadth), 0)
+    line_at = iota((height, breadth), 0)
     first_col = iota((height, LANES), 1) == 0
-    edge = jnp.where(col > 0, message[west, HALO_ROW + 1 : HALO_ROW + 2, :], 0.0)
+    edge = jnp.where(col > 0, row_at(message, west, halo + 1), 0.0)
     left = pltpu.roll(right, 1, 1)
     left = jnp.concatenate(
         [jnp.where(first_col, line_column(geo, edge), left[:, :LANES]), left[:, LANES:]], axis=1
     )
-    edge = jnp.where(row > 0, wide_row(geo, message, north, Y_ROW), 0.0)
-    up = jnp.where(row_at == 0, edge, pltpu.roll(down, 1, 0))
+    edge = jnp.where(row > 0, wide_row(geo, message, north, starts["deep"]), 0.0)
+    up = jnp.where(line_at == 0, edge, pltpu.roll(down, 1, 0))
     diag_top = base_ref[DIAG_T] + left
     diag_low = base_ref[DIAG_B] + up
     planes.update(
@@ -451,8 +477,8 @@
     wide = beside(
         geo,
         top,
-        message[east, HALO_ROW : HALO_ROW + 1, :],
-        message[west, HALO_ROW : HALO_ROW + 1, :],
+        row_at(message, east, halo),
+        row_at(message, west, halo),
     )
     top_out, low_out = matrix(
         geo,
@@ -460,8 +486,8 @@
         top,
         low,
         wide,
-        wide_row(geo, message, north),
-        wide_row(geo, message, south),
+        wide_row(geo, message, north, halo),
+        wide_row(geo, message, south, halo),
     )
     residual_top = source_ref[0] - top_out
     residual_low = source_ref[1] - low_out
@@ -474,17 +500,17 @@
     direction_ref[1] = direction_low
     pull = weight * planes[INV_T]
     lines, spill = shares(geo, weight * direction_top, rel, col)
-    rows = share_rows(lines, spill)
-    rows.update({Y_ROW + i: line for i, line in enumerate(own)})
-    put_all(send, tile_of(rows))
-    lines, spill = shares(geo, weight * pull, rel, col)
-    put_all(send, tile_of(share_rows(lines, spill)), SECOND)
+    square_lines, square_spill = shares(geo, weight * pull, rel, col, 1)
+    starts = rows_of(geo, SECOND)
+    halo = starts["halo"]
+    put_all(send, starts["own"], own + lines + [spill + square_spill] + square_lines)
+    put(send, me, halo, blank(geo))
     below = rel.astype(jnp.float32)
     for target, at in ((east, breadth - 1), (west, 0)):
-        fields = (direction_top, pull, below)
-        put(send, target, HALO_ROW, [column_line(geo, field, at) for field in fields])
-    put(send, north, HALO_ROW, wide_lines(geo, direction_low[:1]))
-    put(send, south, HALO_ROW, wide_lines(geo, direction_low[height - 1 :]))
+        both = column_line(geo, pull, at) + column_line(geo, below, at, LANES // 2)
+        put(send, target, halo, [column_line(geo, direction_top, at), both])
+    put(send, north, halo, wide_lines(geo, direction_low[:1]))
+    put(send, south, halo, wide_lines(geo, direction_low[height - 1 :]))
 
 
 def finish_direction(geo, message, product_ref, row, col, stage, direction, pull, rel):
@@ -508,10 +534,12 @@
     me, east, west, south, north = neighbours(geo, row, col)
     height, breadth = geo.height, geo.breadth
     gain_before = steps_of()[stage - 1][1]
-    gather_own(geo, message, product_ref)
-    gather_shares(geo, message, 0, sums_ref)
+    starts = rows_of(geo, SECOND if stage == 1 else NEXT)
+    halo = starts["halo"]
+    gather_own(geo, message, starts, product_ref)
+    gather_shares(geo, message, starts, sums_ref)
     if stage == 1:
-        gather_shares(geo, message, SECOND, squares_ref)
+        gather_shares(geo, message, starts, squares_ref, "square", 1)
     sums_ref[...] = sums_ref[...] + gain_before * squares_ref[...] * product_ref[...]
     own = own_lines(geo, product(geo, package_ref, sums_ref), own_start(geo, me))
 
@@ -523,14 +551,15 @@
         pull = beside(
             geo,
             weight * state(INV_T),
-            message[east, HALO_ROW + 1 : HALO_ROW + 2, :],
-            message[west, HALO_ROW + 1 : HALO_ROW + 2, :],
+            row_at(message, east, halo + 1),
+            row_at(message, west, halo + 1),
         )
         wide_rel = beside(
             geo,
             rel_ref[...].astype(jnp.float32),
-            message[east, REL_ROW : REL_ROW + 1, :],
-            message[west, REL_ROW : REL_ROW + 1, :],
+            row_at(message, east, halo + 1),
+            row_at(message, west, halo + 1),
+            LANES // 2,
         ).astype(jnp.int32)
         pull_ref[...] = pull
         wide_rel_ref[...] = wide_rel
@@ -541,8 +570,8 @@
     wide = beside(
         geo,
         direction_in[0],
-        message[east, HALO_ROW : HALO_ROW + 1, :],
-        message[west, HALO_ROW : HALO_ROW + 1, :],
+        row_at(message, east, halo),
+        row_at(message, west, halo),
     )
     wide, coupled = finish_direction(
         geo, message, product_ref, row, col, stage - 1, wide, pull, wide_rel
@@ -555,8 +584,8 @@
         top,
         low,
         wide,
-        wide_row(geo, message, north),
-        wide_row(geo, message, south),
+        wide_row(geo, message, north, halo),
+        wide_row(geo, message, south, halo),
     )
     residual_top = residual_in[0] + weight * coupled[:, :breadth] - top_out
     residual_low = residual_in[1] - low_out
@@ -577,14 +606,15 @@
         lines, spill = shares(geo, weight * direction_top, rel, col)
     iterate_ref[0] = iterate_top
     iterate_ref[1] = iterate_low
-    rows = share_rows(lines, spill)
-    rows.update({Y_ROW + i: line for i, line in enumerate(own)})
-    put_all(send, tile_of(rows))
+    starts = rows_of(geo, NEXT if stage < DEG - 1 else LAST)
+    put_all(send, starts["own"], own + lines + [spill])
     if stage < DEG - 1:
-        put(send, east, HALO_ROW, [column_line(geo, direction_top, breadth - 1)])
-        put(send, west, HALO_ROW, [column_line(geo, direction_top, 0)])
-        put(send, north, HALO_ROW, wide_lines(geo, direction_low[:1]))
-        put(send, south, HALO_ROW, wide_lines(geo, direction_low[height - 1 :]))
+        halo = starts["halo"]
+        put(send, me, halo, blank(geo))
+        put(send, east, halo, [column_line(geo, direction_top, breadth - 1)])
+        put(send, west, halo, [column_line(geo, direction_top, 0)])
+        put(send, north, halo, wide_lines(geo, direction_low[:1]))
+        put(send, south, halo, wide_lines(geo, direction_low[height - 1 :]))
 
 
 def last_kernel(
@@ -608,8 +638,9 @@
     me = row * geo.cols + col
     breadth = geo.breadth
     gain = steps_of()[DEG - 1][1]
-    gather_own(geo, message, product_ref)
-    gather_shares(geo, message, 0, sums_ref)
+    starts = rows_of(geo, LAST)
+    gather_own(geo, message, starts, product_ref)
+    gather_shares(geo, message, starts, sums_ref)
     sums_ref[...] = sums_ref[...] + gain * squares_ref[...] * product_ref[...]
     own = own_lines(geo, product(geo, package_ref, sums_ref), 0)
     if geo.own >= LANES:
@@ -692,7 +723,10 @@
     supply = bump_supply.reshape(table)
     field = pltpu.VMEM((height, breadth), f32)
     pair = pltpu.VMEM((2, height, breadth), f32)
-    message = pltpu.VMEM((devices, SUBS, LANES), f32)
+
+    def message(parts):
+        return pltpu.VMEM((devices, 1, rows_of(geo, parts)["end"] * LANES), f32)
+
     held = pltpu.VMEM(table, f32)
 
     whole = pltpu.VMEM((height, breadth), jnp.int32)
@@ -700,7 +734,7 @@
         functools.partial(open_kernel, geo),
         (load_wave,),
         (
-            message,
+            message(FIRST),
             whole,
             pair,
             pltpu.VMEM(package.shape, f32),
@@ -731,7 +765,7 @@
         functools.partial(first_kernel, geo),
         (exchange(sent), package, volt, base, source, rel),
         (
-            pltpu.VMEM((devices, 2 * SUBS, LANES), f32),
+            message(SECOND),
             pltpu.VMEM((10, height, breadth), f32),
             pair,
             pair,
@@ -742,7 +776,7 @@
     sent, residual, direction, iterate, pull, wide_rel, squares = call(
         functools.partial(step_kernel, geo, 1),
         (exchange(sent), package, state, residual, direction, volt, rel),
-        (message, pair, pair, pair, pltpu.VMEM(wide, f32), pltpu.VMEM(wide, jnp.int32), held),
+        (message(NEXT), pair, pair, pair, pltpu.VMEM(wide, f32), pltpu.VMEM(wide, jnp.int32), held),
         (held, held),
     )
     for stage in range(2, DEG):
@@ -759,7 +793,7 @@
                 wide_rel,
                 squares,
             ),
-            (message, pair, pair, pair) if stage < DEG - 1 else (message, pair),
+            (message(NEXT), pair, pair, pair) if stage < DEG - 1 else (message(LAST), pair),
             (held, held),
         )
         if carried:

time: 69.5 us -> 65.8 us (0.947)
  blocking collectives: 58.2 us -> 54.1 us
    all_to_all x5, blocking collectives: 58.2 us -> 54.1 us  [exchange(): lax.all_to_all(message, AXES, split_axis=0, concat_axis=0, tiled=True)]
where the time goes in v2:
time: 65.8 us; the launch traced here: 65.5 us
  blocking collectives  54.1 us (82%)
  Pallas kernels  10 us (15%)
  between operations  1.32 us (2%)
    all_to_all x5, blocking collectives, exchange(): lax.all_to_all(message, AXES, split_axis=0, concat_axis=0, tiled=True)  54.1 us
    pallas_call x6, Pallas kernels, call(): pl.pallas_call(kernel, out_shape=list(outputs), in_specs=specs, out_specs...  10 us

profile of v2, /device:TPU:0, one launch (start us, length us, event | category | flops | bytes accessed | tf_op | source)
XLA Modules:
  0.0 65.5 jit_solution(14026901866073759601)
XLA Ops:
  1.3 3.8 %shard_map.148 = (f32[32,1,896]{2,1,0:T(1,128)S(1)}, s32[32,256]{1,0:T(8,128)S(1)}, f32[2,32,256]{2,1,0:T(8,128)S(1)}, f32[256,8192]{1,0:T(8,128)S(1)}, f32[32,2...) custom-call(s32[32,256]{1,0:T(8,128)} %refs_0_.1, ...), custom_call_target="tpu_custom_call" | custom-call | tf_op jit(solution)/shard_map/pallas_call | solution.py:678
  5.1 15.1 %all_to_all.25.message = f32[32,1,896]{2,1,0:T(1,128)S(1)} all-to-all(f32[32,1,896]{2,1,0:T(1,128)S(1)} %get-tuple-element.32), channel_id=1, replica_groups=mesh['row'=8,'col'=4] {'row','col'}, dimensions={0} | all-to-all | bytes 229376 | tf_op jit(solution)/shard_map/all_to_all | solution.py:665
  20.2 1.2 %shard_map.149 = (f32[32,1,1152]{2,1,0:T(1,128)S(1)}, f32[10,32,256]{2,1,0:T(8,128)S(1)}, f32[2,32,256]{2,1,0:T(8,128)S(1)}, f32[2,32,256]{2,1,0:T(8,128)S(1)}) custom-call(f32[32,1,896]{2,1,0:T(1,128)S(1)} %all_to_all.25.message, f32[256,8192]{1,0:T(8,128)S(1)} %get-tuple-element.33.package_ref.refs_1_, ...), custom_call_target="tpu_custom_call" | custom-call | tf_op jit(solution)/shard_map/pallas_call | solution.py:678
  21.4 10.1 %all_to_all.26.refs_0_ = f32[32,1,1152]{2,1,0:T(1,128)S(1)} all-to-all(f32[32,1,1152]{2,1,0:T(1,128)S(1)} %get-tuple-element.38), channel_id=1, replica_groups=mesh['row'=8,'col'=4] {'row','col'}, dimensions={0} | all-to-all | bytes 294912 | tf_op jit(solution)/shard_map/all_to_all | solution.py:665
  31.5 1.1 %shard_map.150 = (f32[32,1,896]{2,1,0:T(1,128)S(1)}, f32[2,32,256]{2,1,0:T(8,128)S(1)}, f32[2,32,256]{2,1,0:T(8,128)S(1)}, f32[2,32,256]{2,1,0:T(8,128)S(1)}, f3...) custom-call(f32[32,1,1152]{2,1,0:T(1,128)S(1)} %all_to_all.26.refs_0_, ...), custom_call_target="tpu_custom_call" | custom-call | tf_op jit(solution)/shard_map/pallas_call | solution.py:678
  32.6 9.9 %all_to_all.27.refs_0_ = f32[32,1,896]{2,1,0:T(1,128)S(1)} all-to-all(f32[32,1,896]{2,1,0:T(1,128)S(1)} %get-tuple-element.42), channel_id=1, replica_groups=mesh['row'=8,'col'=4] {'row','col'}, dimensions={0} | all-to-all | bytes 229376 | tf_op jit(solution)/shard_map/all_to_all | solution.py:665
  42.5 1.2 %shard_map.151 = (f32[32,1,896]{2,1,0:T(1,128)S(1)}, f32[2,32,256]{2,1,0:T(8,128)S(1)}, f32[2,32,256]{2,1,0:T(8,128)S(1)}, f32[2,32,256]{2,1,0:T(8,128)S(1)}) custom-call(f32[32,1,896]{2,1,0:T(1,128)S(1)} %all_to_all.27.refs_0_, f32[256,8192]{1,0:T(8,128)S(1)} %get-tuple-element.33.package_ref.refs_1_, f32[10,32,256]{2,1,0:T(8,128)S(1)} %get-tuple-element.39.refs_2_, ...), custom_call_target="tpu_custom_call" | custom-call | tf_op jit(solution)/shard_map/pallas_call | solution.py:678
  43.7 9.7 %all_to_all.28.refs_0_ = f32[32,1,896]{2,1,0:T(1,128)S(1)} all-to-all(f32[32,1,896]{2,1,0:T(1,128)S(1)} %get-tuple-element.49), channel_id=1, replica_groups=mesh['row'=8,'col'=4] {'row','col'}, dimensions={0} | all-to-all | bytes 229376 | tf_op jit(solution)/shard_map/all_to_all | solution.py:665
  53.5 1.2 %shard_map.152 = (f32[32,1,640]{2,1,0:T(1,128)S(1)}, f32[2,32,256]{2,1,0:T(8,128)S(1)}) custom-call(f32[32,1,896]{2,1,0:T(1,128)S(1)} %all_to_all.28.refs_0_, f32[256,8192]{1,0:T(8,128)S(1)} %get-tuple-element.33.package_ref.refs_1_, f32[10,32,256]{2,1,0:T(8,128)S(1)} %get-tuple-element.39.refs_2_, f32[2,32,256]{2,1,0:T(8,128)S(1)} %get-tuple-element.50.refs_3_, ...), custom_call_target="tpu_custom_call" | custom-call | tf_op jit(solution)/shard_map/pallas_call | solution.py:678
  54.6 9.3 %all_to_all.29.message = f32[32,1,640]{2,1,0:T(1,128)S(1)} all-to-all(f32[32,1,640]{2,1,0:T(1,128)S(1)} %get-tuple-element.53), channel_id=1, replica_groups=mesh['row'=8,'col'=4] {'row','col'}, dimensions={0} | all-to-all | bytes 163840 | tf_op jit(solution)/shard_map/all_to_all | solution.py:665
  63.9 1.6 %shard_map.153 = (f32[2,32,256]{2,1,0:T(8,128)}, f32[32,256]{1,0:T(8,128)}, f32[2,128]{1,0:T(2,128)}) custom-call(f32[32,1,640]{2,1,0:T(1,128)S(1)} %all_to_all.29.message, f32[256,8192]{1,0:T(8,128)S(1)} %get-tuple-element.33.package_ref.refs_1_, f32[2,32,256]{2,1,0:T(8,128)S(1)} %get-tuple-element.54.iterate_ref, ...), custom_call_target="tpu_custom_call" | custom-call | tf_op jit(solution)/shard_map/pallas_call | solution.py:678

commit v3 on v2

--- a/solution.py
+++ b/solution.py
@@ -26,6 +26,8 @@
 SECOND = ("own", "share", "spill", "square", "halo")
 NEXT = ("own", "share", "spill", "halo")
 LAST = ("own", "share", "spill")
+
+OPENING = 5
 
 (LINK_R, LINK_L, LINK_D, LINK_U, VIA, WEIGHT, DIAG_T, DIAG_B, INV_T, INV_B) = range(10)
 
@@ -262,7 +264,7 @@
 
 
 def product(geo, package_ref, sums_ref):
-    groups = geo.own // SUBS
+    groups = package_ref.shape[0] // SUBS
     totals = [jnp.zeros((SUBS, LANES), jnp.float32) for _ in range(groups)]
     for t in range(geo.lattice // LANES):
         line = jnp.broadcast_to(sums_ref[t : t + 1, :], (SUBS, LANES))
@@ -270,6 +272,10 @@
             block = package_ref[g * SUBS : (g + 1) * SUBS, t * LANES : (t + 1) * LANES]
             totals[g] = totals[g] + block * line
     return totals
+
+
+def products(geo, package_refs, sums_ref):
+    return [total for ref in package_refs for total in product(geo, ref, sums_ref)]
 
 
 def own_lines(geo, totals, start):
@@ -384,6 +390,7 @@
     map_ref, mask_ref, cond_ref, wire_ref, cap_ref, via_ref, load_ref, semaphores = refs[22:]
     early = (map_ref, mask_ref, cond_ref, volt_ref, wire_ref)
     late = (cap_ref, via_ref, load_ref, decap_ref, decap_cond_ref, supply_ref, package_ref)
+    inputs = inputs[:-1] + (inputs[-1].at[: package_ref.shape[0], :],)
     copies = fetch(tuple(zip(inputs, early + late)), semaphores)
     for copy in copies[: len(early)]:
         copy.wait()
@@ -427,6 +434,7 @@
 
 def first_kernel(
     geo,
+    package_in,
     message,
     package_ref,
     volt_ref,
@@ -437,15 +445,22 @@
     state_ref,
     residual_ref,
     direction_ref,
+    package_more_ref,
     sums_ref,
+    semaphore,
 ):
+    rows_here = package_ref.shape[0]
+    more = pltpu.make_async_copy(
+        package_in.at[rows_here : geo.own, :], package_more_ref, semaphore
+    )
+    more.start()
     row, col = place()
     me, east, west, south, north = neighbours(geo, row, col)
     height, breadth = geo.height, geo.breadth
     starts = rows_of(geo, FIRST)
     halo = starts["halo"]
     gather_shares(geo, message, starts, sums_ref)
-    own = own_lines(geo, product(geo, package_ref, sums_ref), own_start(geo, me))
+    totals = product(geo, package_ref, sums_ref)
 
     rel = rel_ref[...]
     top, low = volt_ref[0], volt_ref[1]
@@ -503,7 +518,7 @@
     square_lines, square_spill = shares(geo, weight * pull, rel, col, 1)
     starts = rows_of(geo, SECOND)
     halo = starts["halo"]
-    put_all(send, starts["own"], own + lines + [spill + square_spill] + square_lines)
+    put_all(send, starts["share"], lines + [spill + square_spill] + square_lines)
     put(send, me, halo, blank(geo))
     below = rel.astype(jnp.float32)
     for target, at in ((east, breadth - 1), (west, 0)):
@@ -511,6 +526,9 @@
         put(send, target, halo, [column_line(geo, direction_top, at), both])
     put(send, north, halo, wide_lines(geo, direction_low[:1]))
     put(send, south, halo, wide_lines(geo, direction_low[height - 1 :]))
+    more.wait()
+    totals = totals + product(geo, package_more_ref, sums_ref)
+    put_all(send, starts["own"], own_lines(geo, totals, own_start(geo, me)))
 
 
 def finish_direction(geo, message, product_ref, row, col, stage, direction, pull, rel):
@@ -520,15 +538,16 @@
 
 
 def step_kernel(geo, stage, *refs):
+    package_refs, refs = refs[:2], refs[2:]
     if stage == 1:
-        (message, package_ref, state_ref, residual_in, direction_in, iterate_in, rel_ref) = refs[:7]
-        (send, residual_ref, direction_ref, iterate_ref, pull_ref, wide_rel_ref, squares_ref) = refs[7:14]
+        (message, state_ref, residual_in, direction_in, iterate_in, rel_ref) = refs[:6]
+        (send, residual_ref, direction_ref, iterate_ref, pull_ref, wide_rel_ref, squares_ref) = refs[6:13]
     else:
-        (message, package_ref, state_ref, residual_in, direction_in, iterate_in) = refs[:6]
-        (pull_ref, wide_rel_ref, squares_ref) = refs[6:9]
-        (send, iterate_ref) = refs[9:11]
+        (message, state_ref, residual_in, direction_in, iterate_in) = refs[:5]
+        (pull_ref, wide_rel_ref, squares_ref) = refs[5:8]
+        (send, iterate_ref) = refs[8:10]
         if stage < DEG - 1:
-            (residual_ref, direction_ref) = refs[11:13]
+            (residual_ref, direction_ref) = refs[10:12]
     product_ref, sums_ref = refs[-2:]
     row, col = place()
     me, east, west, south, north = neighbours(geo, row, col)
@@ -541,7 +560,7 @@
     if stage == 1:
         gather_shares(geo, message, starts, squares_ref, "square", 1)
     sums_ref[...] = sums_ref[...] + gain_before * squares_ref[...] * product_ref[...]
-    own = own_lines(geo, product(geo, package_ref, sums_ref), own_start(geo, me))
+    own = own_lines(geo, products(geo, package_refs, sums_ref), own_start(geo, me))
 
     def state(at):
         return state_ref[at]
@@ -619,8 +638,9 @@
 
 def last_kernel(
     geo,
+    package_ref,
+    package_more_ref,
     message,
-    package_ref,
     iterate_ref,
     pull_ref,
     wide_rel_ref,
@@ -642,7 +662,7 @@
     gather_own(geo, message, starts, product_ref)
     gather_shares(geo, message, starts, sums_ref)
     sums_ref[...] = sums_ref[...] + gain * squares_ref[...] * product_ref[...]
-    own = own_lines(geo, product(geo, package_ref, sums_ref), 0)
+    own = own_lines(geo, products(geo, (package_ref, package_more_ref), sums_ref), 0)
     if geo.own >= LANES:
         supply = supply_ref[pl.ds(me * len(own), len(own)), :]
         bump_volt_ref[...] = supply + jnp.concatenate(own, axis=0)
@@ -717,6 +737,7 @@
         lattice,
     )
     devices = rows * cols
+    here = own * OPENING // SUBS // SUBS * SUBS
     f32 = jnp.float32
     table = (lattice // LANES, LANES)
     cond = bump_cond.reshape(table)
@@ -730,14 +751,14 @@
     held = pltpu.VMEM(table, f32)
 
     whole = pltpu.VMEM((height, breadth), jnp.int32)
-    sent, rel, volt, package, decap, decap_cond, supply, base, source = call(
+    sent, rel, volt, package_here, decap, decap_cond, supply, base, source = call(
         functools.partial(open_kernel, geo),
         (load_wave,),
         (
             message(FIRST),
             whole,
             pair,
-            pltpu.VMEM(package.shape, f32),
+            pltpu.VMEM((here, lattice), f32),
             field,
             field,
             held,
@@ -761,21 +782,23 @@
         ),
         scalar=0,
     )
-    sent, state, residual, direction = call(
+    sent, state, residual, direction, package_more = call(
         functools.partial(first_kernel, geo),
-        (exchange(sent), package, volt, base, source, rel),
+        (exchange(sent), package_here, volt, base, source, rel),
         (
             message(SECOND),
             pltpu.VMEM((10, height, breadth), f32),
             pair,
             pair,
+            pltpu.VMEM((own - here, lattice), f32),
         ),
-        (held,),
+        (held, pltpu.SemaphoreType.DMA),
+        outside=(package,),
     )
     wide = (height, breadth + LANES)
     sent, residual, direction, iterate, pull, wide_rel, squares = call(
         functools.partial(step_kernel, geo, 1),
-        (exchange(sent), package, state, residual, direction, volt, rel),
+        (package_here, package_more, exchange(sent), state, residual, direction, volt, rel),
         (message(NEXT), pair, pair, pair, pltpu.VMEM(wide, f32), pltpu.VMEM(wide, jnp.int32), held),
         (held, held),
     )
@@ -783,8 +806,9 @@
         sent, iterate, *carried = call(
             functools.partial(step_kernel, geo, stage),
             (
+                package_here,
+                package_more,
                 exchange(sent),
-                package,
                 state,
                 residual,
                 direction,
@@ -801,8 +825,9 @@
     voltage, decap_volt, bump_volt = call(
         functools.partial(last_kernel, geo),
         (
+            package_here,
+            package_more,
             exchange(sent),
-            package,
             iterate,
             pull,
             wide_rel,

time: 65.8 us -> 66.1 us (level)
  no operation moved by 1% of the time
where the time goes in v3:
time: 66.1 us; the launch traced here: 65.9 us
  blocking collectives  54.1 us (82%)
  Pallas kernels  10.4 us (16%)
  between operations  1.32 us (2%)
    all_to_all x5, blocking collectives, exchange(): lax.all_to_all(message, AXES, split_axis=0, concat_axis=0, tiled=True)  54.1 us
    pallas_call x6, Pallas kernels, call(): pl.pallas_call(kernel, out_shape=list(outputs), in_specs=specs, out_specs...  10.4 us

profile of v3, /device:TPU:0, one launch (start us, length us, event | category | flops | bytes accessed | tf_op | source)
XLA Modules:
  0.0 65.9 jit_solution(724427405001610762)
XLA Ops:
  1.3 2.9 %shard_map.148 = (f32[32,1,896]{2,1,0:T(1,128)S(1)}, s32[32,256]{1,0:T(8,128)S(1)}, f32[2,32,256]{2,1,0:T(8,128)S(1)}, f32[160,8192]{1,0:T(8,128)S(1)}, f32[32,2...) custom-call(s32[32,256]{1,0:T(8,128)} %refs_0_.1, ...), custom_call_target="tpu_custom_call" | custom-call | tf_op jit(solution)/shard_map/pallas_call | solution.py:698
  4.2 15.1 %all_to_all.25.message = f32[32,1,896]{2,1,0:T(1,128)S(1)} all-to-all(f32[32,1,896]{2,1,0:T(1,128)S(1)} %get-tuple-element.34), channel_id=1, replica_groups=mesh['row'=8,'col'=4] {'row','col'}, dimensions={0} | all-to-all | bytes 229376 | tf_op jit(solution)/shard_map/all_to_all | solution.py:685
  19.3 2.5 %shard_map.149 = (f32[32,1,1152]{2,1,0:T(1,128)S(1)}, f32[10,32,256]{2,1,0:T(8,128)S(1)}, f32[2,32,256]{2,1,0:T(8,128)S(1)}, f32[2,32,256]{2,1,0:T(8,128)S(1)}, f32[96,8192]{1,0:T(8,128)S(1)}) custom-call(f32[256,8192]{1,0:T(8,128)} %package_in.1, f32[32,1,896]{2,1,0:T(1,128)S(1)} %all_to_all.25.message, ...), custom_call_target="tpu_custom_call" | custom-call | tf_op jit(solution)/shard_map/pallas_call | solution.py:698
  21.7 10.1 %all_to_all.26.refs_2_ = f32[32,1,1152]{2,1,0:T(1,128)S(1)} all-to-all(f32[32,1,1152]{2,1,0:T(1,128)S(1)} %get-tuple-element.40), channel_id=1, replica_groups=mesh['row'=8,'col'=4] {'row','col'}, dimensions={0} | all-to-all | bytes 294912 | tf_op jit(solution)/shard_map/all_to_all | solution.py:685
  31.9 1.1 %shard_map.150 = (f32[32,1,896]{2,1,0:T(1,128)S(1)}, f32[2,32,256]{2,1,0:T(8,128)S(1)}, f32[2,32,256]{2,1,0:T(8,128)S(1)}, f32[2,32,256]{2,1,0:T(8,128)S(1)}, f3...) custom-call(f32[160,8192]{1,0:T(8,128)S(1)} %get-tuple-element.33.package_ref.refs_0_, ...), custom_call_target="tpu_custom_call" | custom-call | tf_op jit(solution)/shard_map/pallas_call | solution.py:698
  33.0 9.9 %all_to_all.27.refs_2_ = f32[32,1,896]{2,1,0:T(1,128)S(1)} all-to-all(f32[32,1,896]{2,1,0:T(1,128)S(1)} %get-tuple-element.44), channel_id=1, replica_groups=mesh['row'=8,'col'=4] {'row','col'}, dimensions={0} | all-to-all | bytes 229376 | tf_op jit(solution)/shard_map/all_to_all | solution.py:685
  42.9 1.2 %shard_map.151 = (f32[32,1,896]{2,1,0:T(1,128)S(1)}, f32[2,32,256]{2,1,0:T(8,128)S(1)}, f32[2,32,256]{2,1,0:T(8,128)S(1)}, f32[2,32,256]{2,1,0:T(8,128)S(1)}) custom-call(f32[160,8192]{1,0:T(8,128)S(1)} %get-tuple-element.33.package_ref.refs_0_, f32[96,8192]{1,0:T(8,128)S(1)} %get-tuple-element.39.refs_1_.package_more_ref, ...), custom_call_target="tpu_custom_call" | custom-call | tf_op jit(solution)/shard_map/pallas_call | solution.py:698
  44.1 9.7 %all_to_all.28.refs_2_ = f32[32,1,896]{2,1,0:T(1,128)S(1)} all-to-all(f32[32,1,896]{2,1,0:T(1,128)S(1)} %get-tuple-element.51), channel_id=1, replica_groups=mesh['row'=8,'col'=4] {'row','col'}, dimensions={0} | all-to-all | bytes 229376 | tf_op jit(solution)/shard_map/all_to_all | solution.py:685
  53.8 1.2 %shard_map.152 = (f32[32,1,640]{2,1,0:T(1,128)S(1)}, f32[2,32,256]{2,1,0:T(8,128)S(1)}) custom-call(f32[160,8192]{1,0:T(8,128)S(1)} %get-tuple-element.33.package_ref.refs_0_, f32[96,8192]{1,0:T(8,128)S(1)} %get-tuple-element.39.refs_1_.package_more_ref, f32[32,1,896]{2,1,0:T(1,128)S(1)} %all_to_all.28.refs_2_, ...), custom_call_target="tpu_custom_call" | custom-call | tf_op jit(solution)/shard_map/pallas_call | solution.py:698
  55.0 9.3 %all_to_all.29.message = f32[32,1,640]{2,1,0:T(1,128)S(1)} all-to-all(f32[32,1,640]{2,1,0:T(1,128)S(1)} %get-tuple-element.55), channel_id=1, replica_groups=mesh['row'=8,'col'=4] {'row','col'}, dimensions={0} | all-to-all | bytes 163840 | tf_op jit(solution)/shard_map/all_to_all | solution.py:685
  64.3 1.6 %shard_map.153 = (f32[2,32,256]{2,1,0:T(8,128)}, f32[32,256]{1,0:T(8,128)}, f32[2,128]{1,0:T(2,128)}) custom-call(f32[160,8192]{1,0:T(8,128)S(1)} %get-tuple-element.33.package_ref.refs_0_, f32[96,8192]{1,0:T(8,128)S(1)} %get-tuple-element.39.refs_1_.package_more_ref, f32[32,1,640]{2,1,0:T(1,128)S(1)} %all_to_all.29.message, ...), custom_call_target="tpu_custom_call" | custom-call | tf_op jit(solution)/shard_map/pallas_call | solution.py:698

commit v4 on v3

--- a/solution.py
+++ b/solution.py
@@ -27,7 +27,7 @@
 NEXT = ("own", "share", "spill", "halo")
 LAST = ("own", "share", "spill")
 
-OPENING = 5
+OPENING = 7
 
 (LINK_R, LINK_L, LINK_D, LINK_U, VIA, WEIGHT, DIAG_T, DIAG_B, INV_T, INV_B) = range(10)
 

time: 66.1 us -> 65.9 us (level)
  no operation moved by 1% of the time
where the time goes in v4:
time: 65.9 us; the launch traced here: 65.6 us
  blocking collectives  54.1 us (82%)
  Pallas kernels  10.2 us (15%)
  between operations  1.32 us (2%)
    all_to_all x5, blocking collectives, exchange(): lax.all_to_all(message, AXES, split_axis=0, concat_axis=0, tiled=True)  54.1 us
    pallas_call x6, Pallas kernels, call(): pl.pallas_call(kernel, out_shape=list(outputs), in_specs=specs, out_specs...  10.2 us

profile of v4, /device:TPU:0, one launch (start us, length us, event | category | flops | bytes accessed | tf_op | source)
XLA Modules:
  0.0 65.6 jit_solution(9546064149365575469)
XLA Ops:
  1.3 3.5 %shard_map.148 = (f32[32,1,896]{2,1,0:T(1,128)S(1)}, s32[32,256]{1,0:T(8,128)S(1)}, f32[2,32,256]{2,1,0:T(8,128)S(1)}, f32[224,8192]{1,0:T(8,128)S(1)}, f32[32,2...) custom-call(s32[32,256]{1,0:T(8,128)} %refs_0_.1, ...), custom_call_target="tpu_custom_call" | custom-call | tf_op jit(solution)/shard_map/pallas_call | solution.py:698
  4.8 15.1 %all_to_all.25.message = f32[32,1,896]{2,1,0:T(1,128)S(1)} all-to-all(f32[32,1,896]{2,1,0:T(1,128)S(1)} %get-tuple-element.34), channel_id=1, replica_groups=mesh['row'=8,'col'=4] {'row','col'}, dimensions={0} | all-to-all | bytes 229376 | tf_op jit(solution)/shard_map/all_to_all | solution.py:685
  19.9 1.6 %shard_map.149 = (f32[32,1,1152]{2,1,0:T(1,128)S(1)}, f32[10,32,256]{2,1,0:T(8,128)S(1)}, f32[2,32,256]{2,1,0:T(8,128)S(1)}, f32[2,32,256]{2,1,0:T(8,128)S(1)}, f32[32,8192]{1,0:T(8,128)S(1)}) custom-call(f32[256,8192]{1,0:T(8,128)} %package_in.1, f32[32,1,896]{2,1,0:T(1,128)S(1)} %all_to_all.25.message, ...), custom_call_target="tpu_custom_call" | custom-call | tf_op jit(solution)/shard_map/pallas_call | solution.py:698
  21.5 10.1 %all_to_all.26.refs_2_ = f32[32,1,1152]{2,1,0:T(1,128)S(1)} all-to-all(f32[32,1,1152]{2,1,0:T(1,128)S(1)} %get-tuple-element.40), channel_id=1, replica_groups=mesh['row'=8,'col'=4] {'row','col'}, dimensions={0} | all-to-all | bytes 294912 | tf_op jit(solution)/shard_map/all_to_all | solution.py:685
  31.6 1.1 %shard_map.150 = (f32[32,1,896]{2,1,0:T(1,128)S(1)}, f32[2,32,256]{2,1,0:T(8,128)S(1)}, f32[2,32,256]{2,1,0:T(8,128)S(1)}, f32[2,32,256]{2,1,0:T(8,128)S(1)}, f3...) custom-call(f32[224,8192]{1,0:T(8,128)S(1)} %get-tuple-element.33.package_ref.refs_0_, ...), custom_call_target="tpu_custom_call" | custom-call | tf_op jit(solution)/shard_map/pallas_call | solution.py:698
  32.8 9.9 %all_to_all.27.refs_2_ = f32[32,1,896]{2,1,0:T(1,128)S(1)} all-to-all(f32[32,1,896]{2,1,0:T(1,128)S(1)} %get-tuple-element.44), channel_id=1, replica_groups=mesh['row'=8,'col'=4] {'row','col'}, dimensions={0} | all-to-all | bytes 229376 | tf_op jit(solution)/shard_map/all_to_all | solution.py:685
  42.6 1.2 %shard_map.151 = (f32[32,1,896]{2,1,0:T(1,128)S(1)}, f32[2,32,256]{2,1,0:T(8,128)S(1)}, f32[2,32,256]{2,1,0:T(8,128)S(1)}, f32[2,32,256]{2,1,0:T(8,128)S(1)}) custom-call(f32[224,8192]{1,0:T(8,128)S(1)} %get-tuple-element.33.package_ref.refs_0_, f32[32,8192]{1,0:T(8,128)S(1)} %get-tuple-element.39.refs_1_.package_more_ref, ...), custom_call_target="tpu_custom_call" | custom-call | tf_op jit(solution)/shard_map/pallas_call | solution.py:698
  43.9 9.7 %all_to_all.28.refs_2_ = f32[32,1,896]{2,1,0:T(1,128)S(1)} all-to-all(f32[32,1,896]{2,1,0:T(1,128)S(1)} %get-tuple-element.51), channel_id=1, replica_groups=mesh['row'=8,'col'=4] {'row','col'}, dimensions={0} | all-to-all | bytes 229376 | tf_op jit(solution)/shard_map/all_to_all | solution.py:685
  53.6 1.2 %shard_map.152 = (f32[32,1,640]{2,1,0:T(1,128)S(1)}, f32[2,32,256]{2,1,0:T(8,128)S(1)}) custom-call(f32[224,8192]{1,0:T(8,128)S(1)} %get-tuple-element.33.package_ref.refs_0_, f32[32,8192]{1,0:T(8,128)S(1)} %get-tuple-element.39.refs_1_.package_more_ref, f32[32,1,896]{2,1,0:T(1,128)S(1)} %all_to_all.28.refs_2_, ...), custom_call_target="tpu_custom_call" | custom-call | tf_op jit(solution)/shard_map/pallas_call | solution.py:698
  54.8 9.3 %all_to_all.29.message = f32[32,1,640]{2,1,0:T(1,128)S(1)} all-to-all(f32[32,1,640]{2,1,0:T(1,128)S(1)} %get-tuple-element.55), channel_id=1, replica_groups=mesh['row'=8,'col'=4] {'row','col'}, dimensions={0} | all-to-all | bytes 163840 | tf_op jit(solution)/shard_map/all_to_all | solution.py:685
  64.1 1.6 %shard_map.153 = (f32[2,32,256]{2,1,0:T(8,128)}, f32[32,256]{1,0:T(8,128)}, f32[2,128]{1,0:T(2,128)}) custom-call(f32[224,8192]{1,0:T(8,128)S(1)} %get-tuple-element.33.package_ref.refs_0_, f32[32,8192]{1,0:T(8,128)S(1)} %get-tuple-element.39.refs_1_.package_more_ref, f32[32,1,640]{2,1,0:T(1,128)S(1)} %all_to_all.29.message, ...), custom_call_target="tpu_custom_call" | custom-call | tf_op jit(solution)/shard_map/pallas_call | solution.py:698

commit v5 on v2

--- a/solution.py
+++ b/solution.py
@@ -445,7 +445,6 @@
     starts = rows_of(geo, FIRST)
     halo = starts["halo"]
     gather_shares(geo, message, starts, sums_ref)
-    own = own_lines(geo, product(geo, package_ref, sums_ref), own_start(geo, me))
 
     rel = rel_ref[...]
     top, low = volt_ref[0], volt_ref[1]
@@ -503,7 +502,7 @@
     square_lines, square_spill = shares(geo, weight * pull, rel, col, 1)
     starts = rows_of(geo, SECOND)
     halo = starts["halo"]
-    put_all(send, starts["own"], own + lines + [spill + square_spill] + square_lines)
+    put_all(send, starts["share"], lines + [spill + square_spill] + square_lines)
     put(send, me, halo, blank(geo))
     below = rel.astype(jnp.float32)
     for target, at in ((east, breadth - 1), (west, 0)):
@@ -511,6 +510,8 @@
         put(send, target, halo, [column_line(geo, direction_top, at), both])
     put(send, north, halo, wide_lines(geo, direction_low[:1]))
     put(send, south, halo, wide_lines(geo, direction_low[height - 1 :]))
+    own = own_lines(geo, product(geo, package_ref, sums_ref), own_start(geo, me))
+    put_all(send, starts["own"], own)
 
 
 def finish_direction(geo, message, product_ref, row, col, stage, direction, pull, rel):
@@ -541,7 +542,6 @@
     if stage == 1:
         gather_shares(geo, message, starts, squares_ref, "square", 1)
     sums_ref[...] = sums_ref[...] + gain_before * squares_ref[...] * product_ref[...]
-    own = own_lines(geo, product(geo, package_ref, sums_ref), own_start(geo, me))
 
     def state(at):
         return state_ref[at]
@@ -607,7 +607,7 @@
     iterate_ref[0] = iterate_top
     iterate_ref[1] = iterate_low
     starts = rows_of(geo, NEXT if stage < DEG - 1 else LAST)
-    put_all(send, starts["own"], own + lines + [spill])
+    put_all(send, starts["share"], lines + [spill])
     if stage < DEG - 1:
         halo = starts["halo"]
         put(send, me, halo, blank(geo))
@@ -615,6 +615,8 @@
         put(send, west, halo, [column_line(geo, direction_top, 0)])
         put(send, north, halo, wide_lines(geo, direction_low[:1]))
         put(send, south, halo, wide_lines(geo, direction_low[height - 1 :]))
+    own = own_lines(geo, product(geo, package_ref, sums_ref), own_start(geo, me))
+    put_all(send, starts["own"], own)
 
 
 def last_kernel(

time: 65.8 us -> 65.7 us (level)
  no operation moved by 1% of the time
where the time goes in v5:
time: 65.7 us; the launch traced here: 65.4 us
  blocking collectives  54.1 us (82%)
  Pallas kernels  9.96 us (15%)
  between operations  1.32 us (2%)
    all_to_all x5, blocking collectives, exchange(): lax.all_to_all(message, AXES, split_axis=0, concat_axis=0, tiled=True)  54.1 us
    pallas_call x6, Pallas kernels, call(): pl.pallas_call(kernel, out_shape=list(outputs), in_specs=specs, out_specs...  9.96 us

profile of v5, /device:TPU:0, one launch (start us, length us, event | category | flops | bytes accessed | tf_op | source)
XLA Modules:
  0.0 65.4 jit_solution(5225589141270894634)
XLA Ops:
  1.3 3.8 %shard_map.148 = (f32[32,1,896]{2,1,0:T(1,128)S(1)}, s32[32,256]{1,0:T(8,128)S(1)}, f32[2,32,256]{2,1,0:T(8,128)S(1)}, f32[256,8192]{1,0:T(8,128)S(1)}, f32[32,2...) custom-call(s32[32,256]{1,0:T(8,128)} %refs_0_.1, ...), custom_call_target="tpu_custom_call" | custom-call | tf_op jit(solution)/shard_map/pallas_call | solution.py:680
  5.1 15.1 %all_to_all.25.message = f32[32,1,896]{2,1,0:T(1,128)S(1)} all-to-all(f32[32,1,896]{2,1,0:T(1,128)S(1)} %get-tuple-element.32), channel_id=1, replica_groups=mesh['row'=8,'col'=4] {'row','col'}, dimensions={0} | all-to-all | bytes 229376 | tf_op jit(solution)/shard_map/all_to_all | solution.py:667
  20.2 1.1 %shard_map.149 = (f32[32,1,1152]{2,1,0:T(1,128)S(1)}, f32[10,32,256]{2,1,0:T(8,128)S(1)}, f32[2,32,256]{2,1,0:T(8,128)S(1)}, f32[2,32,256]{2,1,0:T(8,128)S(1)}) custom-call(f32[32,1,896]{2,1,0:T(1,128)S(1)} %all_to_all.25.message, f32[256,8192]{1,0:T(8,128)S(1)} %get-tuple-element.33.package_ref.refs_1_, ...), custom_call_target="tpu_custom_call" | custom-call | tf_op jit(solution)/shard_map/pallas_call | solution.py:680
  21.3 10.1 %all_to_all.26.refs_0_ = f32[32,1,1152]{2,1,0:T(1,128)S(1)} all-to-all(f32[32,1,1152]{2,1,0:T(1,128)S(1)} %get-tuple-element.38), channel_id=1, replica_groups=mesh['row'=8,'col'=4] {'row','col'}, dimensions={0} | all-to-all | bytes 294912 | tf_op jit(solution)/shard_map/all_to_all | solution.py:667
  31.4 1.1 %shard_map.150 = (f32[32,1,896]{2,1,0:T(1,128)S(1)}, f32[2,32,256]{2,1,0:T(8,128)S(1)}, f32[2,32,256]{2,1,0:T(8,128)S(1)}, f32[2,32,256]{2,1,0:T(8,128)S(1)}, f3...) custom-call(f32[32,1,1152]{2,1,0:T(1,128)S(1)} %all_to_all.26.refs_0_, ...), custom_call_target="tpu_custom_call" | custom-call | tf_op jit(solution)/shard_map/pallas_call | solution.py:680
  32.6 9.9 %all_to_all.27.refs_0_ = f32[32,1,896]{2,1,0:T(1,128)S(1)} all-to-all(f32[32,1,896]{2,1,0:T(1,128)S(1)} %get-tuple-element.42), channel_id=1, replica_groups=mesh['row'=8,'col'=4] {'row','col'}, dimensions={0} | all-to-all | bytes 229376 | tf_op jit(solution)/shard_map/all_to_all | solution.py:667
  42.4 1.2 %shard_map.151 = (f32[32,1,896]{2,1,0:T(1,128)S(1)}, f32[2,32,256]{2,1,0:T(8,128)S(1)}, f32[2,32,256]{2,1,0:T(8,128)S(1)}, f32[2,32,256]{2,1,0:T(8,128)S(1)}) custom-call(f32[32,1,896]{2,1,0:T(1,128)S(1)} %all_to_all.27.refs_0_, f32[256,8192]{1,0:T(8,128)S(1)} %get-tuple-element.33.package_ref.refs_1_, f32[10,32,256]{2,1,0:T(8,128)S(1)} %get-tuple-element.39.refs_2_, ...), custom_call_target="tpu_custom_call" | custom-call | tf_op jit(solution)/shard_map/pallas_call | solution.py:680
  43.7 9.7 %all_to_all.28.refs_0_ = f32[32,1,896]{2,1,0:T(1,128)S(1)} all-to-all(f32[32,1,896]{2,1,0:T(1,128)S(1)} %get-tuple-element.49), channel_id=1, replica_groups=mesh['row'=8,'col'=4] {'row','col'}, dimensions={0} | all-to-all | bytes 229376 | tf_op jit(solution)/shard_map/all_to_all | solution.py:667
  53.4 1.2 %shard_map.152 = (f32[32,1,640]{2,1,0:T(1,128)S(1)}, f32[2,32,256]{2,1,0:T(8,128)S(1)}) custom-call(f32[32,1,896]{2,1,0:T(1,128)S(1)} %all_to_all.28.refs_0_, f32[256,8192]{1,0:T(8,128)S(1)} %get-tuple-element.33.package_ref.refs_1_, f32[10,32,256]{2,1,0:T(8,128)S(1)} %get-tuple-element.39.refs_2_, f32[2,32,256]{2,1,0:T(8,128)S(1)} %get-tuple-element.50.refs_3_, ...), custom_call_target="tpu_custom_call" | custom-call | tf_op jit(solution)/shard_map/pallas_call | solution.py:680
  54.5 9.3 %all_to_all.29.message = f32[32,1,640]{2,1,0:T(1,128)S(1)} all-to-all(f32[32,1,640]{2,1,0:T(1,128)S(1)} %get-tuple-element.53), channel_id=1, replica_groups=mesh['row'=8,'col'=4] {'row','col'}, dimensions={0} | all-to-all | bytes 163840 | tf_op jit(solution)/shard_map/all_to_all | solution.py:667
  63.8 1.6 %shard_map.153 = (f32[2,32,256]{2,1,0:T(8,128)}, f32[32,256]{1,0:T(8,128)}, f32[2,128]{1,0:T(2,128)}) custom-call(f32[32,1,640]{2,1,0:T(1,128)S(1)} %all_to_all.29.message, f32[256,8192]{1,0:T(8,128)S(1)} %get-tuple-element.33.package_ref.refs_1_, f32[2,32,256]{2,1,0:T(8,128)S(1)} %get-tuple-element.54.iterate_ref, ...), custom_call_target="tpu_custom_call" | custom-call | tf_op jit(solution)/shard_map/pallas_call | solution.py:680

commit v6 on v5

--- a/solution.py
+++ b/solution.py
@@ -644,6 +644,14 @@
     gather_own(geo, message, starts, product_ref)
     gather_shares(geo, message, starts, sums_ref)
     sums_ref[...] = sums_ref[...] + gain * squares_ref[...] * product_ref[...]
+    coupled = spread(
+        geo, product_ref, row, col, wide_rel_ref[:, :breadth], breadth // LANES
+    )
+    low = iterate_ref[1]
+    voltage_ref[0] = iterate_ref[0] + gain * pull_ref[:, :breadth] * coupled
+    voltage_ref[1] = low
+    decap_cond = decap_cond_ref[...]
+    decap_volt_ref[...] = (decap_ref[...] + decap_cond * low) / (1.0 + decap_cond)
     own = own_lines(geo, product(geo, package_ref, sums_ref), 0)
     if geo.own >= LANES:
         supply = supply_ref[pl.ds(me * len(own), len(own)), :]
@@ -653,14 +661,6 @@
         line = jnp.broadcast_to(supply_ref[pl.ds(me // sharers, 1), :], (SUBS, LANES))
         line = lookup(line, (iota((SUBS, LANES), 1) + own_start(geo, me)) % LANES)
         bump_volt_ref[...] = (line[:1] + own[0])[:, : geo.own]
-    coupled = spread(
-        geo, product_ref, row, col, wide_rel_ref[:, :breadth], breadth // LANES
-    )
-    low = iterate_ref[1]
-    voltage_ref[0] = iterate_ref[0] + gain * pull_ref[:, :breadth] * coupled
-    voltage_ref[1] = low
-    decap_cond = decap_cond_ref[...]
-    decap_volt_ref[...] = (decap_ref[...] + decap_cond * low) / (1.0 + decap_cond)
 
 
 def exchange(message):

time: 65.7 us -> 65.6 us (level)
  no operation moved by 1% of the time
where the time goes in v6:
time: 65.6 us; the launch traced here: 65.3 us
  blocking collectives  54.1 us (82%)
  Pallas kernels  9.84 us (15%)
  between operations  1.32 us (2%)
    all_to_all x5, blocking collectives, exchange(): lax.all_to_all(message, AXES, split_axis=0, concat_axis=0, tiled=True)  54.1 us
    pallas_call x6, Pallas kernels, call(): pl.pallas_call(kernel, out_shape=list(outputs), in_specs=specs, out_specs...  9.84 us

profile of v6, /device:TPU:0, one launch (start us, length us, event | category | flops | bytes accessed | tf_op | source)
XLA Modules:
  0.0 65.3 jit_solution(3716266347749671141)
XLA Ops:
  1.3 3.8 %shard_map.148 = (f32[32,1,896]{2,1,0:T(1,128)S(1)}, s32[32,256]{1,0:T(8,128)S(1)}, f32[2,32,256]{2,1,0:T(8,128)S(1)}, f32[256,8192]{1,0:T(8,128)S(1)}, f32[32,2...) custom-call(s32[32,256]{1,0:T(8,128)} %refs_0_.1, ...), custom_call_target="tpu_custom_call" | custom-call | tf_op jit(solution)/shard_map/pallas_call | solution.py:680
  5.1 15.1 %all_to_all.25.message = f32[32,1,896]{2,1,0:T(1,128)S(1)} all-to-all(f32[32,1,896]{2,1,0:T(1,128)S(1)} %get-tuple-element.32), channel_id=1, replica_groups=mesh['row'=8,'col'=4] {'row','col'}, dimensions={0} | all-to-all | bytes 229376 | tf_op jit(solution)/shard_map/all_to_all | solution.py:667
  20.2 1.1 %shard_map.149 = (f32[32,1,1152]{2,1,0:T(1,128)S(1)}, f32[10,32,256]{2,1,0:T(8,128)S(1)}, f32[2,32,256]{2,1,0:T(8,128)S(1)}, f32[2,32,256]{2,1,0:T(8,128)S(1)}) custom-call(f32[32,1,896]{2,1,0:T(1,128)S(1)} %all_to_all.25.message, f32[256,8192]{1,0:T(8,128)S(1)} %get-tuple-element.33.package_ref.refs_1_, ...), custom_call_target="tpu_custom_call" | custom-call | tf_op jit(solution)/shard_map/pallas_call | solution.py:680
  21.3 10.1 %all_to_all.26.refs_0_ = f32[32,1,1152]{2,1,0:T(1,128)S(1)} all-to-all(f32[32,1,1152]{2,1,0:T(1,128)S(1)} %get-tuple-element.38), channel_id=1, replica_groups=mesh['row'=8,'col'=4] {'row','col'}, dimensions={0} | all-to-all | bytes 294912 | tf_op jit(solution)/shard_map/all_to_all | solution.py:667
  31.4 1.1 %shard_map.150 = (f32[32,1,896]{2,1,0:T(1,128)S(1)}, f32[2,32,256]{2,1,0:T(8,128)S(1)}, f32[2,32,256]{2,1,0:T(8,128)S(1)}, f32[2,32,256]{2,1,0:T(8,128)S(1)}, f3...) custom-call(f32[32,1,1152]{2,1,0:T(1,128)S(1)} %all_to_all.26.refs_0_, ...), custom_call_target="tpu_custom_call" | custom-call | tf_op jit(solution)/shard_map/pallas_call | solution.py:680
  32.6 9.9 %all_to_all.27.refs_0_ = f32[32,1,896]{2,1,0:T(1,128)S(1)} all-to-all(f32[32,1,896]{2,1,0:T(1,128)S(1)} %get-tuple-element.42), channel_id=1, replica_groups=mesh['row'=8,'col'=4] {'row','col'}, dimensions={0} | all-to-all | bytes 229376 | tf_op jit(solution)/shard_map/all_to_all | solution.py:667
  42.4 1.2 %shard_map.151 = (f32[32,1,896]{2,1,0:T(1,128)S(1)}, f32[2,32,256]{2,1,0:T(8,128)S(1)}, f32[2,32,256]{2,1,0:T(8,128)S(1)}, f32[2,32,256]{2,1,0:T(8,128)S(1)}) custom-call(f32[32,1,896]{2,1,0:T(1,128)S(1)} %all_to_all.27.refs_0_, f32[256,8192]{1,0:T(8,128)S(1)} %get-tuple-element.33.package_ref.refs_1_, f32[10,32,256]{2,1,0:T(8,128)S(1)} %get-tuple-element.39.refs_2_, ...), custom_call_target="tpu_custom_call" | custom-call | tf_op jit(solution)/shard_map/pallas_call | solution.py:680
  43.7 9.7 %all_to_all.28.refs_0_ = f32[32,1,896]{2,1,0:T(1,128)S(1)} all-to-all(f32[32,1,896]{2,1,0:T(1,128)S(1)} %get-tuple-element.49), channel_id=1, replica_groups=mesh['row'=8,'col'=4] {'row','col'}, dimensions={0} | all-to-all | bytes 229376 | tf_op jit(solution)/shard_map/all_to_all | solution.py:667
  53.4 1.2 %shard_map.152 = (f32[32,1,640]{2,1,0:T(1,128)S(1)}, f32[2,32,256]{2,1,0:T(8,128)S(1)}) custom-call(f32[32,1,896]{2,1,0:T(1,128)S(1)} %all_to_all.28.refs_0_, f32[256,8192]{1,0:T(8,128)S(1)} %get-tuple-element.33.package_ref.refs_1_, f32[10,32,256]{2,1,0:T(8,128)S(1)} %get-tuple-element.39.refs_2_, f32[2,32,256]{2,1,0:T(8,128)S(1)} %get-tuple-element.50.refs_3_, ...), custom_call_target="tpu_custom_call" | custom-call | tf_op jit(solution)/shard_map/pallas_call | solution.py:680
  54.5 9.3 %all_to_all.29.message = f32[32,1,640]{2,1,0:T(1,128)S(1)} all-to-all(f32[32,1,640]{2,1,0:T(1,128)S(1)} %get-tuple-element.53), channel_id=1, replica_groups=mesh['row'=8,'col'=4] {'row','col'}, dimensions={0} | all-to-all | bytes 163840 | tf_op jit(solution)/shard_map/all_to_all | solution.py:667
  63.8 1.5 %shard_map.153 = (f32[2,32,256]{2,1,0:T(8,128)}, f32[32,256]{1,0:T(8,128)}, f32[2,128]{1,0:T(2,128)}) custom-call(f32[32,1,640]{2,1,0:T(1,128)S(1)} %all_to_all.29.message, f32[256,8192]{1,0:T(8,128)S(1)} %get-tuple-element.33.package_ref.refs_1_, f32[2,32,256]{2,1,0:T(8,128)S(1)} %get-tuple-element.54.iterate_ref, ...), custom_call_target="tpu_custom_call" | custom-call | tf_op jit(solution)/shard_map/pallas_call | solution.py:680
